TPU v7x, 32 devices: a whole 2x2x4 slice. The times are simulated.
32 devices in a mesh: section: 8 (over y, x, core), shard: 4 (over z).
Axes of the slice: x: 2, y: 2, z: 4, core: 2. Of those that a mesh axis runs over, the one named last changes fastest.
Arguments:
- tokens: bfloat16 [64, 1024, 512], P(('section', 'shard')), may hold values from -6 to 6
- cotangent: bfloat16 [64, 1024, 512], P(('section', 'shard')), may hold values from -6 to 6
- route: int32 [32, 1024], replicated, may hold values from 0 to 1, as said below
- remask: int32 [32, 1024], replicated, may hold values 0 or 1
- timestep: int32 [32], replicated, may hold values from 0 to 49
- enc_qkv: float32 [512, 1536], P('shard'), may hold values from -0.25 to 0.25
- enc_out: float32 [512, 512], P('shard'), may hold values from -2 to 2
- enc_up: float32 [512, 2048], P('shard'), may hold values from -0.25 to 0.25
- enc_down: float32 [2048, 512], P('shard'), may hold values from -0.125 to 0.125
- enc_gains: float32 [2, 512], P(None, 'shard'), may hold values from 0.5 to 1.5
- enc_shifts: float32 [2, 512], P(None, 'shard'), may hold values from -4 to 4
- dec_qkv: float32 [512, 1536], P('shard'), may hold values from -0.25 to 0.25
- dec_out: float32 [512, 512], P('shard'), may hold values from -2 to 2
- cross_query: float32 [512, 512], P('shard'), may hold values from -0.25 to 0.25
- cross_kv: float32 [512, 1024], P('shard'), may hold values from -0.25 to 0.25
- cross_out: float32 [512, 512], P('shard'), may hold values from -2 to 2
- dec_up: float32 [512, 2048], P('shard'), may hold values from -0.25 to 0.25
- dec_down: float32 [2048, 512], P('shard'), may hold values from -0.125 to 0.125
- dec_gains: float32 [3, 512], P(None, 'shard'), may hold values from 0.5 to 1.5
- dec_shifts: float32 [3, 512], P(None, 'shard'), may hold values from -4 to 4
- time_table: float32 [50, 512], P(None, 'shard'), may hold values from -6 to 6
- mask_embed: float32 [512], P('shard'), may hold values from -6 to 6
Outputs:
- layer_out: bfloat16 [64, 1024, 512], P(('section', 'shard'))
- grad_in: float32 [64, 1024, 512], P(('section', 'shard'))
- grad_enc_qkv: float32 [512, 1536], P('shard')
- grad_enc_out: float32 [512, 512], P('shard')
- grad_enc_up: float32 [512, 2048], P('shard')
- grad_enc_down: float32 [2048, 512], P('shard')
- grad_enc_gains: float32 [2, 512], P(None, 'shard')
- grad_enc_shifts: float32 [2, 512], P(None, 'shard')
- grad_dec_qkv: float32 [512, 1536], P('shard')
- grad_dec_out: float32 [512, 512], P('shard')
- grad_cross_query: float32 [512, 512], P('shard')
- grad_cross_kv: float32 [512, 1024], P('shard')
- grad_cross_out: float32 [512, 512], P('shard')
- grad_dec_up: float32 [512, 2048], P('shard')
- grad_dec_down: float32 [2048, 512], P('shard')
- grad_dec_gains: float32 [3, 512], P(None, 'shard')
- grad_dec_shifts: float32 [3, 512], P(None, 'shard')
- grad_time_table: float32 [50, 512], P(None, 'shard')
- grad_mask_embed: float32 [512], P('shard')
Inputs may be any that keep to these rules, and one draw needn't show every extreme that they name: route is 1 at the first token of every sequence.
All inputs are finite; a program needn't handle non-finite values.
Results may differ from a plain program's by a relative error of at most 0.024.
The roundings to bfloat16 on the way count: a program that leaves them out, or rounds other values in their place, can miss the bound.
Values may be sent and summed in bfloat16 or wider, within the bound.
A program may use at most 320 MiB of HBM per device.

v0:
```python
import jax
import jax.numpy as jnp
from jax import lax
from jax.sharding import PartitionSpec as P

HEADS = 8


EPSILON = 1e-05


def passed_along(array, axis, by):
    size = lax.axis_size(axis)
    pairs = [(i, i + by) for i in range(size) if 0 <= i + by < size]
    return lax.ppermute(array, axis, pairs)


def product(left, right):
    return jnp.dot(left, right, preferred_element_type=jnp.float32)


def product_tn(left, right):
    return lax.dot_general(
        left, right, (((0,), (0,)), ((), ())), preferred_element_type=jnp.float32
    )


def product_nt(left, right):
    return lax.dot_general(
        left, right, (((1,), (1,)), ((), ())), preferred_element_type=jnp.float32
    )


def layer_norm(signal, gain_row, shift_row):
    average = jnp.mean(signal, axis=-1, keepdims=True)
    centred = signal - average
    spread = jnp.mean(centred * centred, axis=-1, keepdims=True)
    return centred * lax.rsqrt(spread + EPSILON) * gain_row.astype(jnp.float32) + shift_row.astype(
        jnp.float32
    )


def norm_back(signal, gain_row, shift_row, upstream):
    _, pullback = jax.vjp(
        layer_norm, signal, gain_row.astype(jnp.float32), shift_row.astype(jnp.float32)
    )
    return pullback(upstream)


def gelu_tanh(signal):
    return jax.nn.gelu(signal, approximate=True)


def gelu_back(signal, upstream):
    _, pullback = jax.vjp(gelu_tanh, signal)
    return pullback(upstream)[0]


def split_heads(matrix):
    return matrix.reshape(matrix.shape[0], HEADS, matrix.shape[1] // HEADS)


def attend_forward(query_rows, key_rows, value_rows):
    row_count, features = query_rows.shape
    block_rows = min(512, row_count)
    scaling = (features // HEADS) ** (-0.5)
    key_heads = split_heads(key_rows)
    value_heads = split_heads(value_rows)

    def one_block(query_block):
        scores = (
            jnp.einsum(
                "qhd,khd->hqk",
                split_heads(query_block),
                key_heads,
                preferred_element_type=jnp.float32,
            )
            * scaling
        )
        peak = jnp.max(scores, axis=-1, keepdims=True)
        exponent = jnp.exp(scores - peak)
        totals = jnp.sum(exponent, axis=-1, keepdims=True)
        weights = (exponent / totals).astype(jnp.bfloat16)
        mixed = jnp.einsum("hqk,khd->qhd", weights, value_heads, preferred_element_type=jnp.float32)
        return (mixed.reshape(block_rows, features), (peak + jnp.log(totals))[..., 0])

    mixed, log_sums = lax.map(
        one_block, query_rows.reshape(row_count // block_rows, block_rows, features)
    )
    return (mixed.reshape(row_count, features), log_sums)


def attend_backward(query_rows, key_rows, value_rows, log_sums, upstream):
    row_count, features = query_rows.shape
    block_rows = min(512, row_count)
    blocks = row_count // block_rows
    scaling = (features // HEADS) ** (-0.5)
    key_heads = split_heads(key_rows)
    value_heads = split_heads(value_rows)

    def one_block(carry, inputs):
        grad_keys, grad_values = carry
        query_block, sums_block, upstream_block = inputs
        query_heads = split_heads(query_block)
        upstream_heads = split_heads(upstream_block)
        scores = (
            jnp.einsum("qhd,khd->hqk", query_heads, key_heads, preferred_element_type=jnp.float32)
            * scaling
        )
        weights = jnp.exp(scores - sums_block[..., None])
        grad_weights = jnp.einsum(
            "qhd,khd->hqk", upstream_heads, value_heads, preferred_element_type=jnp.float32
        )
        inner = jnp.sum(weights * grad_weights, axis=-1, keepdims=True)
        grad_scores = (weights * (grad_weights - inner) * scaling).astype(jnp.bfloat16)
        grad_query = jnp.einsum(
            "hqk,khd->qhd", grad_scores, key_heads, preferred_element_type=jnp.float32
        )
        grad_keys = grad_keys + jnp.einsum(
            "hqk,qhd->khd", grad_scores, query_heads, preferred_element_type=jnp.float32
        )
        grad_values = grad_values + jnp.einsum(
            "hqk,qhd->khd",
            weights.astype(jnp.bfloat16),
            upstream_heads,
            preferred_element_type=jnp.float32,
        )
        return (
            (grad_keys, grad_values),
            grad_query.astype(jnp.bfloat16).reshape(block_rows, features),
        )

    start = jnp.zeros(key_heads.shape, jnp.float32)
    inputs = (
        query_rows.reshape(blocks, block_rows, features),
        log_sums,
        upstream.reshape(blocks, block_rows, features),
    )
    (grad_keys, grad_values), grad_query = lax.scan(one_block, (start, start), inputs)
    key_count = key_rows.shape[0]
    grad_keys = grad_keys.reshape(key_count, features).astype(jnp.bfloat16)
    grad_values = grad_values.reshape(key_count, features).astype(jnp.bfloat16)
    return (grad_query.reshape(row_count, features), grad_keys, grad_values)


def attention_forward(inputs_b, weight_qkv, weight_out):
    features = inputs_b.shape[1]
    joined = product(inputs_b, weight_qkv).astype(jnp.bfloat16)
    mixed, log_sums = attend_forward(
        joined[:, :features], joined[:, features : 2 * features], joined[:, 2 * features :]
    )
    mixed_b = mixed.astype(jnp.bfloat16)
    return (product(mixed_b, weight_out), (joined, mixed_b, log_sums))


def attention_back(inputs_b, weight_qkv, weight_out, saved, upstream):
    joined, mixed_b, log_sums = saved
    features = inputs_b.shape[1]
    upstream_b = upstream.astype(jnp.bfloat16)
    grad_out = product_tn(mixed_b, upstream_b)
    grad_mixed = product_nt(upstream_b, weight_out).astype(jnp.bfloat16)
    grad_query, grad_keys, grad_values = attend_backward(
        joined[:, :features],
        joined[:, features : 2 * features],
        joined[:, 2 * features :],
        log_sums,
        grad_mixed,
    )
    grad_joined = jnp.concatenate([grad_query, grad_keys, grad_values], axis=1)
    return (product_nt(grad_joined, weight_qkv), product_tn(inputs_b, grad_joined), grad_out)


def feed_forward(hidden_b, weight_up, weight_down):
    lifted = product(hidden_b, weight_up)
    active = gelu_tanh(lifted).astype(jnp.bfloat16)
    return (product(active, weight_down), (lifted, active))


def feed_back(hidden_b, weight_up, weight_down, saved, upstream):
    lifted, active = saved
    upstream_b = upstream.astype(jnp.bfloat16)
    grad_down = product_tn(active, upstream_b)
    grad_lifted = gelu_back(lifted, product_nt(upstream_b, weight_down)).astype(jnp.bfloat16)
    return (product_nt(grad_lifted, weight_up), product_tn(hidden_b, grad_lifted), grad_down)


def encoder_forward(source, weights):
    weight_qkv, weight_out, weight_up, weight_down, gains, shifts = weights
    branch, attn_saved = attention_forward(source, weight_qkv, weight_out)
    first = source.astype(jnp.float32) + branch
    hidden = layer_norm(first, gains[0], shifts[0])
    hidden_b = hidden.astype(jnp.bfloat16)
    lifted_branch, ffn_saved = feed_forward(hidden_b, weight_up, weight_down)
    second = hidden + lifted_branch
    memory = layer_norm(second, gains[1], shifts[1])
    return (memory, (attn_saved, first, hidden_b, ffn_saved, second))


def encoder_backward(source, weights, saved, upstream):
    weight_qkv, weight_out, weight_up, weight_down, gains, shifts = weights
    attn_saved, first, hidden_b, ffn_saved, second = saved
    grad_second, gain_two, shift_two = norm_back(second, gains[1], shifts[1], upstream)
    grad_hidden, grad_up, grad_down = feed_back(
        hidden_b, weight_up, weight_down, ffn_saved, grad_second
    )
    grad_first, gain_one, shift_one = norm_back(
        first, gains[0], shifts[0], grad_second + grad_hidden
    )
    grad_source, grad_qkv, grad_out = attention_back(
        source, weight_qkv, weight_out, attn_saved, grad_first
    )
    grads = (
        grad_qkv,
        grad_out,
        grad_up,
        grad_down,
        jnp.stack([gain_one, gain_two]),
        jnp.stack([shift_one, shift_two]),
    )
    return (grad_first + grad_source, grads)


def decoder_forward(target, key_values, mask_row, step_row, weights):
    (
        weight_qkv,
        weight_out,
        weight_query,
        weight_kv,
        weight_cross,
        weight_up,
        weight_down,
        gains,
        shifts,
        table,
        mask_vector,
    ) = weights
    features = target.shape[1]
    chosen = lax.dynamic_index_in_dim(table, step_row, 0, keepdims=False).astype(jnp.float32)
    embedded = (
        jnp.where(
            mask_row[:, None] == 1,
            mask_vector.astype(jnp.float32)[None, :],
            target.astype(jnp.float32),
        )
        + chosen[None, :]
    )
    embedded_b = embedded.astype(jnp.bfloat16)
    branch, attn_saved = attention_forward(embedded_b, weight_qkv, weight_out)
    first = embedded + branch
    hidden = layer_norm(first, gains[0], shifts[0])
    hidden_b = hidden.astype(jnp.bfloat16)
    query_b = product(hidden_b, weight_query).astype(jnp.bfloat16)
    mixed, log_sums = attend_forward(query_b, key_values[:, :features], key_values[:, features:])
    mixed_b = mixed.astype(jnp.bfloat16)
    second = hidden + product(mixed_b, weight_cross)
    middle = layer_norm(second, gains[1], shifts[1])
    middle_b = middle.astype(jnp.bfloat16)
    lifted_branch, ffn_saved = feed_forward(middle_b, weight_up, weight_down)
    third = middle + lifted_branch
    result = layer_norm(third, gains[2], shifts[2])
    return (
        result,
        (
            embedded_b,
            attn_saved,
            first,
            hidden_b,
            query_b,
            mixed_b,
            log_sums,
            second,
            middle_b,
            ffn_saved,
            third,
        ),
    )


def decoder_backward(target, key_values, mask_row, step_row, weights, upstream):
    (
        weight_qkv,
        weight_out,
        weight_query,
        weight_kv,
        weight_cross,
        weight_up,
        weight_down,
        gains,
        shifts,
        table,
        mask_vector,
    ) = weights
    features = target.shape[1]
    _, saved = decoder_forward(target, key_values, mask_row, step_row, weights)
    (
        embedded_b,
        attn_saved,
        first,
        hidden_b,
        query_b,
        mixed_b,
        log_sums,
        second,
        middle_b,
        ffn_saved,
        third,
    ) = saved
    grad_third, gain_three, shift_three = norm_back(third, gains[2], shifts[2], upstream)
    grad_middle, grad_up, grad_down = feed_back(
        middle_b, weight_up, weight_down, ffn_saved, grad_third
    )
    grad_second, gain_two, shift_two = norm_back(
        second, gains[1], shifts[1], grad_third + grad_middle
    )
    second_b = grad_second.astype(jnp.bfloat16)
    grad_cross = product_tn(mixed_b, second_b)
    grad_mixed = product_nt(second_b, weight_cross).astype(jnp.bfloat16)
    grad_query, grad_keys, grad_values = attend_backward(
        query_b, key_values[:, :features], key_values[:, features:], log_sums, grad_mixed
    )
    grad_weight_query = product_tn(hidden_b, grad_query)
    grad_hidden = grad_second + product_nt(grad_query, weight_query)
    grad_first, gain_one, shift_one = norm_back(first, gains[0], shifts[0], grad_hidden)
    grad_embed_attn, grad_qkv, grad_out = attention_back(
        embedded_b, weight_qkv, weight_out, attn_saved, grad_first
    )
    grad_embedded = grad_first + grad_embed_attn
    masked = mask_row[:, None] == 1
    grad_target = jnp.where(masked, 0.0, grad_embedded)
    grad_mask = jnp.sum(jnp.where(masked, grad_embedded, 0.0), axis=0)
    picked = (jnp.arange(table.shape[0]) == step_row).astype(jnp.float32)
    grad_table = picked[:, None] * jnp.sum(grad_embedded, axis=0)[None, :]
    grad_key_values = jnp.concatenate([grad_keys, grad_values], axis=1)
    grads = (
        grad_qkv,
        grad_out,
        grad_weight_query,
        jnp.zeros(weight_kv.shape, jnp.float32),
        grad_cross,
        grad_up,
        grad_down,
        jnp.stack([gain_one, gain_two, gain_three]),
        jnp.stack([shift_one, shift_two, shift_three]),
        grad_table,
        grad_mask,
    )
    return (grad_target, grads, grad_key_values)


def reduce_grads(grads):
    owned = (
        lax.psum_scatter(
            grads[0].astype(jnp.bfloat16), "shard", scatter_dimension=0, tiled=True
        ).astype(jnp.float32),
        lax.psum_scatter(
            grads[1].astype(jnp.bfloat16), "shard", scatter_dimension=0, tiled=True
        ).astype(jnp.float32),
        lax.psum_scatter(
            grads[2].astype(jnp.bfloat16), "shard", scatter_dimension=0, tiled=True
        ).astype(jnp.float32),
        lax.psum_scatter(
            grads[3].astype(jnp.bfloat16), "shard", scatter_dimension=0, tiled=True
        ).astype(jnp.float32),
        lax.psum_scatter(
            grads[4].astype(jnp.bfloat16), "shard", scatter_dimension=1, tiled=True
        ).astype(jnp.float32),
        lax.psum_scatter(
            grads[5].astype(jnp.bfloat16), "shard", scatter_dimension=1, tiled=True
        ).astype(jnp.float32),
        lax.psum_scatter(
            grads[6].astype(jnp.bfloat16), "shard", scatter_dimension=0, tiled=True
        ).astype(jnp.float32),
        lax.psum_scatter(
            grads[7].astype(jnp.bfloat16), "shard", scatter_dimension=0, tiled=True
        ).astype(jnp.float32),
        lax.psum_scatter(
            grads[8].astype(jnp.bfloat16), "shard", scatter_dimension=0, tiled=True
        ).astype(jnp.float32),
        lax.psum_scatter(
            grads[9].astype(jnp.bfloat16), "shard", scatter_dimension=0, tiled=True
        ).astype(jnp.float32),
        lax.psum_scatter(
            grads[10].astype(jnp.bfloat16), "shard", scatter_dimension=0, tiled=True
        ).astype(jnp.float32),
        lax.psum_scatter(
            grads[11].astype(jnp.bfloat16), "shard", scatter_dimension=0, tiled=True
        ).astype(jnp.float32),
        lax.psum_scatter(
            grads[12].astype(jnp.bfloat16), "shard", scatter_dimension=0, tiled=True
        ).astype(jnp.float32),
        lax.psum_scatter(
            grads[13].astype(jnp.bfloat16), "shard", scatter_dimension=1, tiled=True
        ).astype(jnp.float32),
        lax.psum_scatter(
            grads[14].astype(jnp.bfloat16), "shard", scatter_dimension=1, tiled=True
        ).astype(jnp.float32),
        lax.psum_scatter(
            grads[15].astype(jnp.bfloat16), "shard", scatter_dimension=1, tiled=True
        ).astype(jnp.float32),
        lax.psum_scatter(
            grads[16].astype(jnp.bfloat16), "shard", scatter_dimension=0, tiled=True
        ).astype(jnp.float32),
    )
    return lax.psum(
        (
            owned[0],
            owned[1],
            owned[2],
            owned[3],
            owned[4],
            owned[5],
            owned[6],
            owned[7],
            owned[8],
            owned[9],
            owned[10],
            owned[11],
            owned[12],
            owned[13],
            owned[14],
            owned[15],
            owned[16],
        ),
        "section",
    )


def per_device(
    tokens,
    cotangent,
    route,
    remask,
    timestep,
    enc_qkv,
    enc_out,
    enc_up,
    enc_down,
    enc_gains,
    enc_shifts,
    dec_qkv,
    dec_out,
    cross_query,
    cross_kv,
    cross_out,
    dec_up,
    dec_down,
    dec_gains,
    dec_shifts,
    time_table,
    mask_embed,
):
    halfway = lax.axis_size("section") // 2
    shards = lax.axis_size("shard")
    section_index = lax.axis_index("section")
    is_decoder = section_index >= halfway
    batches = tokens.shape[0]
    length = tokens.shape[1]
    features = tokens.shape[2]
    first_row = (
        jnp.maximum(section_index - halfway, 0) * shards + lax.axis_index("shard")
    ) * batches
    mask_rows = lax.dynamic_slice_in_dim(remask, first_row, batches, 0)
    step_rows = lax.dynamic_slice_in_dim(timestep, first_row, batches, 0)
    route_rows = lax.dynamic_slice_in_dim(route, first_row, batches, 0).astype(jnp.float32)
    counts = jnp.sum(route.reshape(-1, batches, length).astype(jnp.float32), axis=(0, 2))
    total_tokens = float(route.shape[0] // batches * length)
    scale_rows = route_rows * total_tokens / counts[:, None]
    full = (
        lax.all_gather(enc_qkv.astype(jnp.bfloat16), "shard", axis=0, tiled=True),
        lax.all_gather(enc_out.astype(jnp.bfloat16), "shard", axis=0, tiled=True),
        lax.all_gather(enc_up.astype(jnp.bfloat16), "shard", axis=0, tiled=True),
        lax.all_gather(enc_down.astype(jnp.bfloat16), "shard", axis=0, tiled=True),
        lax.all_gather(enc_gains.astype(jnp.bfloat16), "shard", axis=1, tiled=True),
        lax.all_gather(enc_shifts.astype(jnp.bfloat16), "shard", axis=1, tiled=True),
        lax.all_gather(dec_qkv.astype(jnp.bfloat16), "shard", axis=0, tiled=True),
        lax.all_gather(dec_out.astype(jnp.bfloat16), "shard", axis=0, tiled=True),
        lax.all_gather(cross_query.astype(jnp.bfloat16), "shard", axis=0, tiled=True),
        lax.all_gather(cross_kv.astype(jnp.bfloat16), "shard", axis=0, tiled=True),
        lax.all_gather(cross_out.astype(jnp.bfloat16), "shard", axis=0, tiled=True),
        lax.all_gather(dec_up.astype(jnp.bfloat16), "shard", axis=0, tiled=True),
        lax.all_gather(dec_down.astype(jnp.bfloat16), "shard", axis=0, tiled=True),
        lax.all_gather(dec_gains.astype(jnp.bfloat16), "shard", axis=1, tiled=True),
        lax.all_gather(dec_shifts.astype(jnp.bfloat16), "shard", axis=1, tiled=True),
        lax.all_gather(time_table.astype(jnp.bfloat16), "shard", axis=1, tiled=True),
        lax.all_gather(mask_embed.astype(jnp.bfloat16), "shard", axis=0, tiled=True),
    )
    enc_weights = full[:6]
    dec_weights = full[6:]
    weight_kv = full[9]
    back_type = jnp.float32

    def send_forward(payload):
        return passed_along(payload, "section", halfway)

    def keys_from(received):
        return product(received, weight_kv).astype(jnp.bfloat16)

    def back_from(received, grad_key_values):
        return (product_tn(received, grad_key_values), product_nt(grad_key_values, weight_kv))

    def send_back(payload):
        return passed_along(payload, "section", -halfway)

    def memory_term(returned):
        return (returned, jnp.zeros(weight_kv.shape, jnp.float32))

    def encode(source):
        memory, _ = encoder_forward(source, enc_weights)
        memory_b = memory.astype(jnp.bfloat16)
        return (memory_b, memory_b)

    def skip_encode(source):
        return (
            jnp.zeros((length, features), jnp.bfloat16),
            jnp.zeros((length, features), jnp.bfloat16),
        )

    def decode(operand):
        target, received, mask_row, step_row = operand
        result, _ = decoder_forward(target, keys_from(received), mask_row, step_row, dec_weights)
        return result.astype(jnp.bfloat16)

    def skip_decode(operand):
        return jnp.zeros((length, features), jnp.bfloat16)

    def forward_step(carry, inputs):
        source, mask_row, step_row = inputs
        memory_b, payload = lax.cond(is_decoder, skip_encode, encode, source)
        received = send_forward(payload)
        result_b = lax.cond(is_decoder, decode, skip_decode, (source, received, mask_row, step_row))
        return (carry, (jnp.where(is_decoder, result_b, memory_b), received))

    _, (layer_out, kept) = lax.scan(
        forward_step, jnp.zeros((), jnp.float32), (tokens, mask_rows, step_rows)
    )

    def decode_back(operand):
        target, received, mask_row, step_row, upstream = operand
        grad_target, grads, grad_key_values = decoder_backward(
            target, keys_from(received), mask_row, step_row, dec_weights, upstream
        )
        grad_weight_kv, payload = back_from(received, grad_key_values)
        return (grad_target, grads[:3] + (grad_weight_kv,) + grads[4:], payload)

    def skip_decode_back(operand):
        blank_grads = tuple((jnp.zeros(weight.shape, jnp.float32) for weight in dec_weights))
        return (
            jnp.zeros((length, features), jnp.float32),
            blank_grads,
            jnp.zeros((length, features), back_type),
        )

    def encode_back(operand):
        source, upstream, returned = operand
        memory, saved = encoder_forward(source, enc_weights)
        term, extra = memory_term(returned)
        grad_source, grads = encoder_backward(
            source, enc_weights, saved, upstream.astype(jnp.float32) + term
        )
        return (grad_source, grads, extra)

    def skip_encode_back(operand):
        blank_grads = tuple((jnp.zeros(weight.shape, jnp.float32) for weight in enc_weights))
        return (
            jnp.zeros((length, features), jnp.float32),
            blank_grads,
            jnp.zeros(weight_kv.shape, jnp.float32),
        )

    start = tuple((jnp.zeros(weight.shape, jnp.float32) for weight in full))

    def gather_up(running, local):
        return tuple((left + right for left, right in zip(running, local)))

    def backward_step(running, inputs):
        source, upstream, scale_row, mask_row, step_row, received = inputs
        dec_upstream = upstream.astype(jnp.float32) * scale_row[:, None]
        grad_target, dec_grads, payload = lax.cond(
            is_decoder,
            decode_back,
            skip_decode_back,
            (source, received, mask_row, step_row, dec_upstream),
        )
        returned = send_back(payload)
        grad_source, enc_grads, extra = lax.cond(
            is_decoder, skip_encode_back, encode_back, (source, upstream, returned)
        )
        local = enc_grads + dec_grads[:3] + (dec_grads[3] + extra,) + dec_grads[4:]
        return (gather_up(running, local), jnp.where(is_decoder, grad_target, grad_source))

    running, grad_in = lax.scan(
        backward_step, start, (tokens, cotangent, scale_rows, mask_rows, step_rows, kept)
    )
    return (layer_out, grad_in) + tuple(reduce_grads(running))


def solution(mesh):
    return jax.shard_map(
        per_device,
        mesh=mesh,
        in_specs=(
            P(("section", "shard"), None, None),
            P(("section", "shard"), None, None),
            P(),
            P(),
            P(),
            P("shard", None),
            P("shard", None),
            P("shard", None),
            P("shard", None),
            P(None, "shard"),
            P(None, "shard"),
            P("shard", None),
            P("shard", None),
            P("shard", None),
            P("shard", None),
            P("shard", None),
            P("shard", None),
            P("shard", None),
            P(None, "shard"),
            P(None, "shard"),
            P(None, "shard"),
            P("shard"),
        ),
        out_specs=(
            P(("section", "shard"), None, None),
            P(("section", "shard"), None, None),
            P("shard", None),
            P("shard", None),
            P("shard", None),
            P("shard", None),
            P(None, "shard"),
            P(None, "shard"),
            P("shard", None),
            P("shard", None),
            P("shard", None),
            P("shard", None),
            P("shard", None),
            P("shard", None),
            P("shard", None),
            P(None, "shard"),
            P(None, "shard"),
            P(None, "shard"),
            P("shard"),
        ),
        check_vma=False,
    )
```

profile of v0, /device:TPU:0, one launch (start us, length us, event | category | flops | bytes accessed | tf_op | source)
XLA Modules:
  0.0 2649.7 jit_solution(7213903587936486482)
XLA Ops:
  184.7 46.7 %all-gather.13.cloned.1.call-done = bf16[2048,512]{1,0:T(8,128)(2,1)} async-done(((bf16[512,512]{1,0:T(8,128)(2,1)}), bf16[2048,512]{1,0:T(8,128)(2,1)}) %all-gather.13.cloned.1.call-update) | async-done | bytes 2097168 | tf_op jit(solution)/shard_map/all_gather | solution.py:472
  231.3 46.7 %all-gather.19.cloned.1.call-done = bf16[512,2048]{1,0:T(8,128)(2,1)} async-done(((bf16[128,2048]{1,0:T(8,128)(2,1)}), bf16[512,2048]{1,0:T(8,128)(2,1)}) %all-gather.19.cloned.1.call-update) | async-done | bytes 2097168 | tf_op jit(solution)/shard_map/all_gather | solution.py:480
  278.0 46.3 %all-gather.21.cloned.1.call-done = bf16[2048,512]{1,0:T(8,128)(2,1)} async-done(((bf16[512,512]{1,0:T(8,128)(2,1)}), bf16[2048,512]{1,0:T(8,128)(2,1)}) %all-gather.21.cloned.1.call-update) | async-done | bytes 2097168 | tf_op jit(solution)/shard_map/all_gather | solution.py:481
  324.3 256.7 %while.221 = (s32[]{:T(128)}, bf16[2,1024,512]{2,1,0:T(8,128)(2,1)}, bf16[2,1024,512]{2,1,0:T(8,128)(2,1)}, pred[]{:T(512)}, bf16[2,1024,512]{1,2,0:T(8,128)(2,1...) while((s32[]{:T(128)}, bf16[2,1024,512]{2,1,0:T(8,128)(2,1)}, ...), condition=%wide.region_27.28_spmd, body=%wide.region_0.27_spmd.sunk | while | flops 18396233728 | bytes 284566304 | solution.py:533
  327.0 59.9 %conditional.10 = (bf16[1024,512]{0,1:T(8,128)(2,1)S(1)}) conditional(s32[]{:T(128)} %convert_element_type.853, (bf16[1024,512]{0,1:T(8,128)(2,1)}, bf16[512,1536]{1,0:T(8,128)(2,1)S(1)}, bf16[512,512]{1,0:T(8,128)(2,1)}, bf16[2,512]{1,0:T(2,128)(2,1)}, bf16[2,512]{1,0:T(2,128)(2,1)}, /*index=5*/bf16[512,2048]{1,0:T(8,128)(2,1)}, ...), branch_computations={%region_1.9_spmd, %region_10.10_spmd} | conditional | flops 7570723840 | bytes 88207568 | solution.py:528
  333.8 39.1 %while.218 = (s32[]{:T(128)}, bf16[2,512,512]{2,1,0:T(8,128)(2,1)}, bf16[2,512,512]{2,1,0:T(8,128)(2,1)S(1)}, bf16[1024,8,64]{0,2,1:T(8,128)(2,1)}, bf16[1024,8,64]{0,2,1:T(8,128)(2,1)}, /*index=5*/s32[]{:T(128)}) while((s32[]{:T(128)}, bf16[2,512,512]{2,1,0:T(8,128)(2,1)}, bf16[2,512,512]{2,1,0:T(8,128)(2,1)S(1)}, ...), condition=%wide.region_5.4_spmd, body=%wide.region_2.3_spmd.sunk | while | flops 1094714368 | bytes 40927316 | solution.py:87
  422.2 59.6 %conditional.10 = (bf16[1024,512]{0,1:T(8,128)(2,1)S(1)}) conditional(s32[]{:T(128)} %convert_element_type.853, (bf16[1024,512]{0,1:T(8,128)(2,1)}, bf16[512,1536]{1,0:T(8,128)(2,1)S(1)}, bf16[512,512]{1,0:T(8,128)(2,1)}, bf16[2,512]{1,0:T(2,128)(2,1)}, bf16[2,512]{1,0:T(2,128)(2,1)}, /*index=5*/bf16[512,2048]{1,0:T(8,128)(2,1)}, ...), branch_computations={%region_1.9_spmd, %region_10.10_spmd} | conditional | flops 7570723840 | bytes 88207568 | solution.py:528
  429.0 39.2 %while.218 = (s32[]{:T(128)}, bf16[2,512,512]{2,1,0:T(8,128)(2,1)}, bf16[2,512,512]{2,1,0:T(8,128)(2,1)S(1)}, bf16[1024,8,64]{0,2,1:T(8,128)(2,1)}, bf16[1024,8,64]{0,2,1:T(8,128)(2,1)}, /*index=5*/s32[]{:T(128)}) while((s32[]{:T(128)}, bf16[2,512,512]{2,1,0:T(8,128)(2,1)}, bf16[2,512,512]{2,1,0:T(8,128)(2,1)S(1)}, ...), condition=%wide.region_5.4_spmd, body=%wide.region_2.3_spmd.sunk | while | flops 1094714368 | bytes 40927316 | solution.py:87
  482.4 68.5 %collective-permute-start.1 = (bf16[1024,512]{1,0:T(8,128)(2,1)S(1)}, bf16[1024,512]{1,0:T(8,128)(2,1)}, u32[]{:S(2)}, u32[]{:S(2)}) collective-permute-start(bf16[1024,512]{1,0:T(8,128)(2,1)S(1)} %copy.334), channel_id=1, source_target_pairs={{0,16},{4,20},{8,24},{12,28},{1,17},{5,21},{9,25},{13,29},{2,18},{... | collective-permute-start | bytes 3145736 | tf_op jit(solution)/shard_map/while/body/eval_jaxpr/ppermute | solution.py:15
  581.0 1438.3 %while.222 = (s32[]{:T(128)}, f32[512,1536]{0,1:T(8,128)}, f32[512,512]{1,0:T(8,128)}, f32[512,2048]{1,0:T(8,128)}, f32[2048,512]{1,0:T(8,128)}, /*index=5*/f32[...) while((s32[]{:T(128)}, f32[512,1536]{0,1:T(8,128)}, ...), condition=%wide.region_88.89_spmd.clone, body=%wide.region_30.88_spmd.clone.sunk | while | flops 56998379520 | bytes 1893161984 | solution.py:591
  635.0 572.8 %collective-permute-done = f32[1024,512]{0,1:T(8,128)S(1)} collective-permute-done((f32[1024,512]{0,1:T(8,128)}, f32[1024,512]{0,1:T(8,128)S(1)}, u32[]{:S(2)}, u32[]{:S(2)}) %collective-permute-start) | collective-permute-done | bytes 2097184 | tf_op jit(solution)/shard_map/while/body/eval_jaxpr/ppermute | solution.py:15
  1209.1 232.8 %conditional.13 = (f32[1024,512]{0,1:T(8,128)S(1)}, f32[512,1536]{0,1:T(8,128)S(1)}, f32[512,512]{1,0:T(8,128)}, f32[512,2048]{1,0:T(8,128)}, f32[2048,512]{1,0:...) conditional(s32[]{:T(128)} %convert_element_type.854, (bf16[1024,512]{0,1:T(8,128)(2,1)}, ...), branch_computations={%region_67.86_spmd.clone, %region_87.87_spmd.clone} | conditional | flops 23319040000 | bytes 488609824 | solution.py:585
  1219.8 25.1 while.216
  1284.9 143.7 %while.217 = (s32[]{:T(128)}, f32[1024,8,64]{0,2,1:T(8,128)}, f32[1024,8,64]{0,2,1:T(8,128)}, bf16[2,512,512]{2,1,0:T(8,128)(2,1)}, bf16[2,512,512]{1,2,0:T(8,12...) while((s32[]{:T(128)}, f32[1024,8,64]{0,2,1:T(8,128)}, ...), condition=%wide.region_82.81_spmd.clone, body=%wide.region_80.80_spmd.clone.sunk | while | flops 2741250048 | bytes 203997360 | solution.py:139
  1305.5 25.5 fusion.456
  1377.3 25.5 fusion.456
  1402.7 23.8 bitcast_add_fusion.12
  1513.6 239.1 %collective-permute-done = f32[1024,512]{0,1:T(8,128)S(1)} collective-permute-done((f32[1024,512]{0,1:T(8,128)}, f32[1024,512]{0,1:T(8,128)S(1)}, u32[]{:S(2)}, u32[]{:S(2)}) %collective-permute-start) | collective-permute-done | bytes 2097184 | tf_op jit(solution)/shard_map/while/body/eval_jaxpr/ppermute | solution.py:15
  1754.0 232.9 %conditional.13 = (f32[1024,512]{0,1:T(8,128)S(1)}, f32[512,1536]{0,1:T(8,128)S(1)}, f32[512,512]{1,0:T(8,128)}, f32[512,2048]{1,0:T(8,128)}, f32[2048,512]{1,0:...) conditional(s32[]{:T(128)} %convert_element_type.854, (bf16[1024,512]{0,1:T(8,128)(2,1)}, ...), branch_computations={%region_67.86_spmd.clone, %region_87.87_spmd.clone} | conditional | flops 23319040000 | bytes 488609824 | solution.py:585
  1764.9 25.0 while.216
  1829.7 143.9 %while.217 = (s32[]{:T(128)}, f32[1024,8,64]{0,2,1:T(8,128)}, f32[1024,8,64]{0,2,1:T(8,128)}, bf16[2,512,512]{2,1,0:T(8,128)(2,1)}, bf16[2,512,512]{1,2,0:T(8,12...) while((s32[]{:T(128)}, f32[1024,8,64]{0,2,1:T(8,128)}, ...), condition=%wide.region_82.81_spmd.clone, body=%wide.region_80.80_spmd.clone.sunk | while | flops 2741250048 | bytes 203997360 | solution.py:139
  1850.6 25.5 fusion.456
  1922.3 25.5 fusion.456
  1947.8 23.8 bitcast_add_fusion.12
  2210.4 28.3 %reduce-scatter.41.cloned.1.call-done = bf16[128,1024]{1,0:T(8,128)(2,1)} async-done(((bf16[512,1024]{1,0:T(8,128)(2,1)}), bf16[128,1024]{1,0:T(8,128)(2,1)}) %reduce-scatter.41.cloned.1.call-update) | async-done | bytes 262160 | tf_op jit(solution)/shard_map/reduce_scatter | solution.py:379
  2238.7 36.1 %reduce-scatter.27.cloned.1.call-done = bf16[128,1536]{1,0:T(8,128)(2,1)} async-done(((bf16[512,1536]{1,0:T(8,128)(2,1)}), bf16[128,1536]{1,0:T(8,128)(2,1)}) %reduce-scatter.27.cloned.1.call-update) | async-done | bytes 393232 | tf_op jit(solution)/shard_map/reduce_scatter | solution.py:352
  2274.9 36.6 %reduce-scatter.35.cloned.1.call-done = bf16[128,1536]{1,0:T(8,128)(2,1)} async-done(((bf16[512,1536]{1,0:T(8,128)(2,1)}), bf16[128,1536]{1,0:T(8,128)(2,1)}) %reduce-scatter.35.cloned.1.call-update) | async-done | bytes 393232 | tf_op jit(solution)/shard_map/reduce_scatter | solution.py:370
  2311.5 45.0 %reduce-scatter.31.cloned.1.call-done = bf16[128,2048]{1,0:T(8,128)(2,1)} async-done(((bf16[512,2048]{1,0:T(8,128)(2,1)}), bf16[128,2048]{1,0:T(8,128)(2,1)}) %reduce-scatter.31.cloned.1.call-update) | async-done | bytes 524304 | tf_op jit(solution)/shard_map/reduce_scatter | solution.py:358
  2356.5 45.6 %reduce-scatter.33.cloned.1.call-done = bf16[512,512]{1,0:T(8,128)(2,1)} async-done(((bf16[2048,512]{1,0:T(8,128)(2,1)}), bf16[512,512]{1,0:T(8,128)(2,1)}) %reduce-scatter.33.cloned.1.call-update) | async-done | bytes 524304 | tf_op jit(solution)/shard_map/reduce_scatter | solution.py:361
  2402.1 45.5 %reduce-scatter.45.cloned.1.call-done = bf16[128,2048]{1,0:T(8,128)(2,1)} async-done(((bf16[512,2048]{1,0:T(8,128)(2,1)}), bf16[128,2048]{1,0:T(8,128)(2,1)}) %reduce-scatter.45.cloned.1.call-update) | async-done | bytes 524304 | tf_op jit(solution)/shard_map/reduce_scatter | solution.py:385
  2447.6 45.6 %reduce-scatter.47.cloned.1.call-done = bf16[512,512]{1,0:T(8,128)(2,1)} async-done(((bf16[2048,512]{1,0:T(8,128)(2,1)}), bf16[512,512]{1,0:T(8,128)(2,1)}) %reduce-scatter.47.cloned.1.call-update) | async-done | bytes 524304 | tf_op jit(solution)/shard_map/reduce_scatter | solution.py:388
  2493.2 149.8 %all-reduce.3 = (f32[128,1536]{1,0:T(8,128)}, f32[128,512]{1,0:T(8,128)}, f32[128,2048]{1,0:T(8,128)}, f32[512,512]{1,0:T(8,128)}, f32[2,128]{1,0:T(2,128)}, /*i...) all-reduce(bf16[128,1536]{1,0:T(8,128)(2,1)} %reduce-scatter.27.clo, ...), channel_id=1, replica_groups=mesh['section'=8,'shard'=4] {'section'}, use_global_device_ids=true, to_apply=%region_90.91 | all-reduce | flops 1842816 | bytes 11057152 | tf_op jit(solution)/shard_map/psum | solution.py:404
  (821 shorter events, 1037.4 us)
Async XLA Ops:
  7.2 156.7 %all-gather.17.cloned.1.call-start = ((), (), s32[]{:S(2)}) async-start(), calls=%async_computation.20 | async-start | bytes 1310720 | tf_op jit(solution)/shard_map/all_gather | solution.py:478
  9.2 154.7 %all-gather.9.cloned.1.call-start = ((), (), s32[]{:S(2)}) async-start(), calls=%async_computation.16 | async-start | bytes 1966080 | tf_op jit(solution)/shard_map/all_gather | solution.py:469
  11.2 152.7 %all-gather.15.cloned.1.call-start = ((), (), s32[]{:S(2)}) async-start(), calls=%async_computation.19 | async-start | bytes 1966080 | tf_op jit(solution)/shard_map/all_gather | solution.py:475
  12.1 172.6 %all-gather.11.cloned.1.call-start = ((), (), s32[]{:S(2)}) async-start(), calls=%async_computation.17 | async-start | bytes 2621440 | tf_op jit(solution)/shard_map/all_gather | solution.py:471
  13.0 218.3 %all-gather.13.cloned.1.call-start = ((), (), s32[]{:S(2)}) async-start(), calls=%async_computation.18 | async-start | bytes 2621440 | tf_op jit(solution)/shard_map/all_gather | solution.py:472
  14.0 264.0 %all-gather.19.cloned.1.call-start = ((), (), s32[]{:S(2)}) async-start(), calls=%async_computation.21 | async-start | bytes 2621440 | tf_op jit(solution)/shard_map/all_gather | solution.py:480
  15.0 309.3 %all-gather.21.cloned.1.call-start = ((), (), s32[]{:S(2)}) async-start(), calls=%async_computation.22 | async-start | bytes 2621440 | tf_op jit(solution)/shard_map/all_gather | solution.py:481
  17.3 2050.7 %reduce-scatter.51.cloned.1.call-start = ((), (), s32[]{:S(2)}) async-start(), calls=%async_computation.35 | async-start | bytes 163840
  387.5 24.0 collective-permute-start.1
  482.4 89.3 %collective-permute-start.1 = (bf16[1024,512]{1,0:T(8,128)(2,1)S(1)}, bf16[1024,512]{1,0:T(8,128)(2,1)}, u32[]{:S(2)}, u32[]{:S(2)}) collective-permute-start(bf16[1024,512]{1,0:T(8,128)(2,1)S(1)} %copy.334), channel_id=1, source_target_pairs={{0,16},{4,20},{8,24},{12,28},{1,17},{5,21},{9,25},{13,29},{2,18},{... | collective-permute-start | bytes 3145736 | tf_op jit(solution)/shard_map/while/body/eval_jaxpr/ppermute | solution.py:15
  614.8 593.0 %collective-permute-start = (f32[1024,512]{0,1:T(8,128)}, f32[1024,512]{0,1:T(8,128)S(1)}, u32[]{:S(2)}, u32[]{:S(2)}) collective-permute-start(f32[1024,512]{0,1:T(8,128)} %get-tuple-element.3136), channel_id=1, source_target_pairs={{16,0},{20,4},{24,8},{28,12},{17,1},{21,5},{25,9},{29,13},{18,2},{... | collective-permute-start | bytes 6291464 | tf_op jit(solution)/shard_map/while/body/eval_jaxpr/ppermute | solution.py:15
  629.8 579.3 %copy-start.45 = (bf16[1024,512]{0,1:T(8,128)(2,1)S(1)}, bf16[1024,512]{0,1:T(8,128)(2,1)}, u32[]{:S(2)}) copy-start(bf16[1024,512]{0,1:T(8,128)(2,1)} %copy-done.44) | copy-start | bytes 3145732 | tf_op jit(solution)/shard_map/while
  635.0 574.1 %copy-start.25 = (f32[2048,512]{1,0:T(8,128)}, f32[2048,512]{1,0:T(8,128)S(1)}, u32[]{:S(2)}) copy-start(f32[2048,512]{1,0:T(8,128)S(1)} %select_add_fusion.43) | copy-start | bytes 12582916 | tf_op jit(solution)/shard_map/while
  1493.0 259.7 %collective-permute-start = (f32[1024,512]{0,1:T(8,128)}, f32[1024,512]{0,1:T(8,128)S(1)}, u32[]{:S(2)}, u32[]{:S(2)}) collective-permute-start(f32[1024,512]{0,1:T(8,128)} %get-tuple-element.3136), channel_id=1, source_target_pairs={{16,0},{20,4},{24,8},{28,12},{17,1},{21,5},{25,9},{29,13},{18,2},{... | collective-permute-start | bytes 6291464 | tf_op jit(solution)/shard_map/while/body/eval_jaxpr/ppermute | solution.py:15
  1508.4 245.6 %copy-start.45 = (bf16[1024,512]{0,1:T(8,128)(2,1)S(1)}, bf16[1024,512]{0,1:T(8,128)(2,1)}, u32[]{:S(2)}) copy-start(bf16[1024,512]{0,1:T(8,128)(2,1)} %copy-done.44) | copy-start | bytes 3145732 | tf_op jit(solution)/shard_map/while
  1513.6 240.4 %copy-start.25 = (f32[2048,512]{1,0:T(8,128)}, f32[2048,512]{1,0:T(8,128)S(1)}, u32[]{:S(2)}) copy-start(f32[2048,512]{1,0:T(8,128)S(1)} %select_add_fusion.43) | copy-start | bytes 12582916 | tf_op jit(solution)/shard_map/while
  2021.0 47.9 %reduce-scatter.49.cloned.1.call-start = ((), (), s32[]{:S(2)}) async-start(), calls=%async_computation.34 | async-start | bytes 163840
  2022.6 57.0 %reduce-scatter.55.cloned.1.call-start = ((), (), s32[]{:S(2)}) async-start(), calls=%async_computation.37 | async-start | bytes 163840
  2024.2 75.6 %reduce-scatter.53.cloned.1.call-start = ((), (), s32[]{:S(2)}) async-start(), calls=%async_computation.36 | async-start | bytes 163840
  2025.8 93.6 %reduce-scatter.57.cloned.1.call-start = ((), (), s32[]{:S(2)}) async-start(), calls=%async_computation.38 | async-start | bytes 163840
  2027.5 114.5 %reduce-scatter.29.cloned.1.call-start = ((), (), s32[]{:S(2)}) async-start(), calls=%async_computation.24 | async-start | bytes 655360 | tf_op jit(solution)/shard_map/reduce_scatter | solution.py:355
  2029.7 135.2 %reduce-scatter.37.cloned.1.call-start = ((), (), s32[]{:S(2)}) async-start(), calls=%async_computation.28 | async-start | bytes 655360 | tf_op jit(solution)/shard_map/reduce_scatter | solution.py:373
  2030.6 157.0 %reduce-scatter.39.cloned.1.call-start = ((), (), s32[]{:S(2)}) async-start(), calls=%async_computation.29 | async-start | bytes 655360 | tf_op jit(solution)/shard_map/reduce_scatter | solution.py:376
  2033.0 177.5 %reduce-scatter.43.cloned.1.call-start = ((), (), s32[]{:S(2)}) async-start(), calls=%async_computation.31 | async-start | bytes 655360 | tf_op jit(solution)/shard_map/reduce_scatter | solution.py:382
  2033.9 204.8 %reduce-scatter.41.cloned.1.call-start = ((), (), s32[]{:S(2)}) async-start(), calls=%async_computation.30 | async-start | bytes 1310720 | tf_op jit(solution)/shard_map/reduce_scatter | solution.py:379
  2035.1 239.7 %reduce-scatter.27.cloned.1.call-start = ((), (), s32[]{:S(2)}) async-start(), calls=%async_computation.23 | async-start | bytes 1966080 | tf_op jit(solution)/shard_map/reduce_scatter | solution.py:352
  2038.4 273.0 %reduce-scatter.35.cloned.1.call-start = ((), (), s32[]{:S(2)}) async-start(), calls=%async_computation.27 | async-start | bytes 1966080 | tf_op jit(solution)/shard_map/reduce_scatter | solution.py:370
  2039.8 316.6 %reduce-scatter.31.cloned.1.call-start = ((), (), s32[]{:S(2)}) async-start(), calls=%async_computation.25 | async-start | bytes 2621440 | tf_op jit(solution)/shard_map/reduce_scatter | solution.py:358
  2043.7 358.3 %reduce-scatter.33.cloned.1.call-start = ((), (), s32[]{:S(2)}) async-start(), calls=%async_computation.26 | async-start | bytes 2621440 | tf_op jit(solution)/shard_map/reduce_scatter | solution.py:361
  2047.6 400.0 %reduce-scatter.45.cloned.1.call-start = ((), (), s32[]{:S(2)}) async-start(), calls=%async_computation.32 | async-start | bytes 2621440 | tf_op jit(solution)/shard_map/reduce_scatter | solution.py:385
  2051.6 441.6 %reduce-scatter.47.cloned.1.call-start = ((), (), s32[]{:S(2)}) async-start(), calls=%async_computation.33 | async-start | bytes 2621440 | tf_op jit(solution)/shard_map/reduce_scatter | solution.py:388
  2055.5 587.4 %copy-start.1 = (s32[32,1024]{1,0:T(8,128)S(1)}, s32[32,1024]{1,0:T(8,128)}, u32[]{:S(2)}) copy-start(s32[32,1024]{1,0:T(8,128)} %param.55) | copy-start | bytes 393220
  (189 other events, 841.4 us)
Sparse Core Ops, SparseCore 0:
  10.2 30.6 all-gather.16
  42.5 38.7 all-gather.8
  82.8 50.5 all-gather.14
  135.5 49.1 all-gather.10
  186.7 44.6 all-gather.12
  233.3 44.6 all-gather.18
  279.6 44.6 all-gather.20
  2021.1 18.0 reduce-scatter.50
  2042.1 17.2 reduce-scatter.48
  2062.1 17.4 reduce-scatter.54
  2082.5 17.1 reduce-scatter.52
  2101.8 17.4 reduce-scatter.56
  2122.3 19.7 reduce-scatter.28
  2144.8 19.9 reduce-scatter.36
  2167.6 19.9 reduce-scatter.38
  2190.4 19.9 reduce-scatter.42
  2213.2 25.4 reduce-scatter.40
  2240.9 33.9 reduce-scatter.26
  2277.2 34.2 reduce-scatter.34
  2313.6 42.8 reduce-scatter.30
  2358.9 43.1 reduce-scatter.32
  2404.4 43.1 reduce-scatter.44
  2450.0 43.1 reduce-scatter.46
where the time goes:
time: 2660 us; the launch traced here: 2650 us
  waiting for transfers between devices  1440 us (54%)
  matrix products  476 us (18%)
  blocking collectives  299 us (11%)
  local copies, waits for them, and re-layouts  179 us (7%)
  other arithmetic  133 us (5%)
  starting transfers between devices  74.4 us (3%)
  loops' own time  37 us (1%)
    ppermute x4, waiting for transfers between devices, passed_along(): return lax.ppermute(array, axis, pairs)  854 us
    psum x1, blocking collectives, reduce_grads(): lax.psum((owned[0], owned[1], owned[2], owned[3], owned[4], owned[5], own...  150 us
    dot_general x4, matrix products, one_block(): jnp.einsum('hqk,khd->qhd', grad_scores, key_heads, preferred_element_type...  102 us
    dot_general x4, matrix products, one_block(): jnp.einsum('hqk,qhd->khd', grad_scores, query_heads, preferred_element_ty...  93.8 us
    ppermute x4, starting transfers between devices, passed_along(): return lax.ppermute(array, axis, pairs)  73.4 us
  transfers between devices with their start and end apart: 27, of which 22 were waited for; matrix products, arithmetic and copies ran while one was open for 3% of the time, Pallas kernels for 0%

commit v1 on v0

v1 whole, which is shorter than its diff:
```python
import functools

import jax
import jax.numpy as jnp
from jax import lax
from jax.experimental import pallas as pl
from jax.experimental.pallas import tpu as pltpu
from jax.sharding import PartitionSpec as P

HEADS = 8
EPSILON = 1e-05
BF = jnp.bfloat16
F32 = jnp.float32
NN = (((1,), (0,)), ((), ()))
NT = (((1,), (1,)), ((), ()))
TN = (((0,), (0,)), ((), ()))
RB = 256
LANES = 128
WIDTH = 512
MASK_ROW = 10
STEP_ROW = 11
VEC_ROWS = 12


def dot(left, right, dims=NN):
    return lax.dot_general(left, right, dims, preferred_element_type=F32)


def rows_at(r, count=RB):
    return pl.ds(pl.multiple_of(r * count, count), count)


def lanes_at(c, count=LANES):
    return pl.ds(pl.multiple_of(c * count, count), count)


def low_half(shape):
    return lax.broadcasted_iota(jnp.int32, shape, 1) < LANES // 2


def norm_rows(value):
    average = jnp.mean(value, axis=-1, keepdims=True)
    centred = value - average
    spread = jnp.mean(centred * centred, axis=-1, keepdims=True)
    inverse = lax.rsqrt(spread + EPSILON)
    return centred * inverse, inverse


def norm_rows_back(upstream, normal, inverse, gain):
    scaled = upstream * gain
    first = jnp.mean(scaled, axis=-1, keepdims=True)
    second = jnp.mean(scaled * normal, axis=-1, keepdims=True)
    return inverse * (scaled - first - normal * second)


def gelu_both(p):
    a = 0.7978845608028654
    b = 0.044715
    square = p * p
    t = jnp.tanh(p * (a + (a * b) * square))
    half = 0.5 + 0.5 * t
    slope = half + (0.5 * p) * (1.0 - t * t) * (a + (3.0 * a * b) * square)
    return p * half, slope


def kernel(
    x_in, cot_in, aux, vec, wa, wu, wd,
    lo, gin, ga, gu, gd, gacc, p_hbm, f_hbm,
    x, qkv, oa, xh, rs, hb, res, dfb, dob, cotb, big, dp, kvt, gs, gsd,
    x_sem, cot_sem, big_sem, gs_sem, gsd_sem, lo_sem, gin_sem,
):
    length, features = x.shape[1], x.shape[2]
    hidden = wu.shape[2]
    blocks = length // RB
    pairs = features // LANES
    width = features
    section = lax.axis_index("section")
    role = (section >= lax.axis_size("section") // 2).astype(jnp.int32)
    own, other = role, 1 - role

    def for_rows(body):
        def step(r, carry):
            body(rows_at(r))
            return carry

        lax.fori_loop(0, blocks, step, 0)

    def embed(layer):
        flag = layer.astype(F32)

        def body(rows):
            source = x[layer, rows, :].astype(F32)
            masked = aux[rows, 0:1] * flag > 0.5
            value = jnp.where(masked, vec[MASK_ROW], source) + vec[STEP_ROW] * flag
            res[layer, rows, :] = value
            x[layer, rows, :] = value.astype(BF)

        for_rows(body)

    def project(source, weight, target, first, last):
        for c in range(first, last):
            cols = slice(c * width, (c + 1) * width)

            def body(rows, cols=cols):
                target[rows, cols] = dot(source[rows, :], weight[:, cols]).astype(BF)

            for_rows(body)

    slots = big.shape[0]

    def attend(which):
        source, target, saved = qkv.at[which], oa.at[which], p_hbm.at[which]
        steps = pairs * blocks

        def store(t):
            slot = lax.rem(t, slots)
            return pltpu.make_async_copy(big.at[slot], saved.at[t], big_sem.at[slot])

        def step(t, carry):
            hp, qb = t // blocks, lax.rem(t, blocks)
            slot = lax.rem(t, slots)
            rows = rows_at(qb)
            q = source[rows, lanes_at(hp)] * jnp.asarray(0.125, BF)
            k = source[:, lanes_at(pairs + hp)]
            v = source[:, lanes_at(2 * pairs + hp)]

            @pl.when(t >= slots)
            def _():
                store(t - slots).wait()

            low = low_half((RB, LANES))
            zero = jnp.zeros_like(q)
            parts = []
            for j in range(2):
                s = dot(jnp.where(low if j == 0 else ~low, q, zero), k, NT)
                e = jnp.exp(s - jnp.max(s, axis=-1, keepdims=True))
                total = jnp.sum(e, axis=-1, keepdims=True)
                weights = (e * (1.0 / total)).astype(BF)
                for h in range(2):
                    big[slot, (2 * j + h) * RB : (2 * j + h + 1) * RB, :] = weights[:, h * width : (h + 1) * width]
                parts.append(dot(weights, v))
            target[rows, lanes_at(hp)] = jnp.where(low, parts[0], parts[1]).astype(BF)
            store(t).start()
            return carry

        lax.fori_loop(0, steps, step, 0)
        for t in range(steps - slots, steps):
            store(t).wait()

    def out_norm(which, res_at, xh_at, gain_row, shift_row, hb_at):
        def body(rows):
            value = dot(oa[which, rows, :], wa[which, :, 3 * width :]) + res[res_at, rows, :]
            normal, inverse = norm_rows(value)
            result = normal * vec[gain_row] + vec[shift_row]
            xh[xh_at, rows, :] = normal.astype(BF)
            rs[xh_at, rows, :] = inverse
            res[res_at, rows, :] = result
            hb[hb_at, rows, :] = result.astype(BF)

        for_rows(body)

    chunks = hidden // width

    def feed_store(layer, c):
        slot = c % 2
        return pltpu.make_async_copy(big.at[2 * slot : 2 * slot + 2], f_hbm.at[layer, c], big_sem.at[slot])

    def feed_load(layer, c):
        slot = c % 2
        return pltpu.make_async_copy(f_hbm.at[layer, c], big.at[2 * slot : 2 * slot + 2], big_sem.at[slot])

    def feed(layer, hb_at):
        for c in range(chunks):
            slot = c % 2
            cols = slice(c * width, (c + 1) * width)
            if c >= 2:
                feed_store(layer, c - 2).wait()

            def body(rows, slot=slot, cols=cols):
                value, slope = gelu_both(dot(hb[hb_at, rows, :], wu[layer, :, cols]))
                value = value.astype(BF)
                big[2 * slot, rows, :] = value
                big[2 * slot + 1, rows, :] = slope.astype(BF)
                res[layer, rows, :] += dot(value, wd[layer, cols, :])

            for_rows(body)
            feed_store(layer, c).start()
        for c in range(chunks - 2, chunks):
            feed_store(layer, c).wait()

    def final_norm(layer, xh_at, gain_row, shift_row, target):
        def body(rows):
            normal, inverse = norm_rows(res[layer, rows, :])
            xh[xh_at, rows, :] = normal.astype(BF)
            rs[xh_at, rows, :] = inverse
            target[rows, :] = (normal * vec[gain_row] + vec[shift_row]).astype(BF)

        for_rows(body)

    def norm_back(load, res_at, xh_at, gain_row, shift_row):
        def body(rows):
            upstream = load(rows)
            normal = xh[xh_at, rows, :].astype(F32)
            result = norm_rows_back(upstream, normal, rs[xh_at, rows, :], vec[gain_row])
            gacc[gain_row] += jnp.sum(upstream * normal, axis=0, keepdims=True)
            gacc[shift_row] += jnp.sum(upstream, axis=0, keepdims=True)
            res[res_at, rows, :] = result
            dfb[rows, :] = result.astype(BF)

        for_rows(body)

    def feed_back(layer, hb_at, up, down):
        feed_load(layer, 0).start()
        feed_load(layer, 1).start()
        for c in range(chunks):
            slot = c % 2
            cols = slice(c * width, (c + 1) * width)
            feed_load(layer, c).wait()

            def body(rows, slot=slot, cols=cols):
                grad = dot(dfb[rows, :], wd[layer, cols, :], NT)
                grad = (grad * big[2 * slot + 1, rows, :].astype(F32)).astype(BF)
                dp[rows, :] = grad
                res[layer, rows, :] += dot(grad, wu[layer, :, cols], NT)

            for_rows(body)
            up[:, cols] = dot(hb[hb_at], dp[...], TN).astype(BF)
            down[cols, :] = dot(big[2 * slot], dfb[...], TN).astype(BF)
            if c + 2 < chunks:
                feed_load(layer, c + 2).start()

    def attend_back(which):
        source, output, saved = qkv.at[which], oa.at[which], p_hbm.at[which]
        steps = pairs * blocks

        def fetch(t):
            slot = lax.rem(t, slots)
            return pltpu.make_async_copy(saved.at[t], big.at[slot], big_sem.at[slot])

        for t in range(slots - 1):
            fetch(t).start()

        def step(t, carry):
            hp, qb = t // blocks, lax.rem(t, blocks)
            slot = lax.rem(t, slots)
            rows = rows_at(qb)

            @pl.when(t + slots - 1 < steps)
            def _():
                fetch(t + slots - 1).start()

            fetch(t).wait()

            @pl.when(qb == 0)
            def _():
                kvt[...] = jnp.zeros_like(kvt)

            q = source[rows, lanes_at(hp)]
            k = source[:, lanes_at(pairs + hp)]
            v = source[:, lanes_at(2 * pairs + hp)]
            do = dob[rows, lanes_at(hp)]
            inner = do.astype(F32) * output[rows, lanes_at(hp)].astype(F32)
            low = low_half((RB, LANES))
            zero = jnp.zeros_like(q)
            parts = []
            for j in range(2):
                mine = low if j == 0 else ~low
                dom = jnp.where(mine, do, zero)
                delta = jnp.sum(jnp.where(mine, inner, 0.0), axis=-1, keepdims=True)
                weights = jnp.concatenate(
                    [big[slot, (2 * j + h) * RB : (2 * j + h + 1) * RB, :] for h in range(2)], axis=1
                )
                ds = (weights.astype(F32) * (dot(dom, v, NT) - delta)).astype(BF)
                kvt[1] += dot(dom, weights, TN)
                kvt[0] += dot(jnp.where(mine, q, zero), ds, TN)
                parts.append(dot(ds, k))
            source[rows, lanes_at(hp)] = (jnp.where(low, parts[0], parts[1]) * 0.125).astype(BF)

            @pl.when(qb == blocks - 1)
            def _():
                source[:, lanes_at(pairs + hp)] = jnp.transpose(kvt[0] * 0.125).astype(BF)
                source[:, lanes_at(2 * pairs + hp)] = jnp.transpose(kvt[1]).astype(BF)

            return carry

        lax.fori_loop(0, steps, step, 0)

    def grad_weight(target, first, last, left, which):
        for c in range(first, last):
            cols = slice(c * width, (c + 1) * width)
            target[:, cols] = dot(left[...], qkv[which, :, cols], TN).astype(BF)

    def out_back(which, target):
        target[:, 3 * width :] = dot(oa[which], dfb[...], TN).astype(BF)

        def body(rows):
            dob[rows, :] = dot(dfb[rows, :], wa[which, :, 3 * width :], NT).astype(BF)

        for_rows(body)

    load_x = pltpu.make_async_copy(x_in, x, x_sem)
    load_x.start()
    load_x.wait()
    gacc[...] = jnp.zeros_like(gacc)

    for layer in (own, other):
        embed(layer)
        project(x.at[layer], wa.at[layer], qkv.at[layer], 0, 3)
        attend(layer)
        out_norm(layer, layer, layer, 4 * layer, 2 + 5 * layer, layer)

    feed(0, 0)
    final_norm(0, 2, 1, 3, hb.at[2])
    send_memory = pltpu.make_async_copy(hb.at[2], lo.at[0], lo_sem.at[0])
    send_memory.start()
    load_cot = pltpu.make_async_copy(cot_in.at[1], cotb, cot_sem.at[1])
    load_cot.start()
    project(hb.at[1], wa.at[2], qkv.at[2], 0, 1)
    project(hb.at[2], wa.at[2], qkv.at[2], 1, 3)
    attend(2)
    out_norm(2, 1, 3, 5, 8, 3)
    feed(1, 3)
    final_norm(1, 4, 6, 9, dob)
    send_result = pltpu.make_async_copy(dob, lo.at[1], lo_sem.at[1])
    send_result.start()

    def result_upstream(rows):
        return cotb[rows, :].astype(F32) * aux[rows, 1:2]

    load_cot.wait()
    norm_back(result_upstream, 1, 4, 6, 9)
    load_cot = pltpu.make_async_copy(cot_in.at[0], cotb, cot_sem.at[0])
    load_cot.start()
    feed_back(1, 3, gs.at[0], gsd)
    store_up = pltpu.make_async_copy(gs.at[0], gu.at[1], gs_sem.at[0])
    store_down = pltpu.make_async_copy(gsd, gd.at[1], gsd_sem)
    store_up.start()
    store_down.start()
    norm_back(lambda rows: res[1, rows, :], 1, 3, 5, 8)
    send_result.wait()
    out_back(2, gs.at[1])
    attend_back(2)
    grad_weight(gs.at[1], 0, 1, hb.at[1], 2)
    grad_weight(gs.at[1], 1, 3, hb.at[2], 2)
    store_cross = pltpu.make_async_copy(gs.at[1], ga.at[2], gs_sem.at[1])
    store_cross.start()
    load_cot.wait()

    def cross_body(rows):
        res[1, rows, :] += dot(qkv[2, rows, :width], wa[2, :, :width], NT)
        res[0, rows, :] = cotb[rows, :].astype(F32) + dot(
            qkv[2, rows, width:], wa[2, :, width : 3 * width], NT
        )

    for_rows(cross_body)
    norm_back(lambda rows: res[0, rows, :], 0, 2, 1, 3)
    store_up.wait()
    store_down.wait()
    feed_back(0, 0, gs.at[0], gsd)
    store_up = pltpu.make_async_copy(gs.at[0], gu.at[0], gs_sem.at[0])
    store_down = pltpu.make_async_copy(gsd, gd.at[0], gsd_sem)
    store_up.start()
    store_down.start()
    store_cross.wait()
    for turn, layer in enumerate((other, own)):
        slot = 1 - turn
        flag = layer.astype(F32)
        norm_back(lambda rows: res[layer, rows, :], layer, layer, 4 * layer, 2 + 5 * layer)
        if turn == 1:
            store_up.wait()
        out_back(layer, gs.at[slot])
        attend_back(layer)
        grad_weight(gs.at[slot], 0, 3, x.at[layer], layer)
        pltpu.make_async_copy(gs.at[slot], ga.at[layer], gs_sem.at[slot]).start()

        def body(rows):
            value = res[layer, rows, :] + dot(qkv[layer, rows, :], wa[layer, :, : 3 * width], NT)
            masked = aux[rows, 0:1] * flag > 0.5
            gacc[MASK_ROW] += jnp.sum(jnp.where(masked, value, 0.0), axis=0, keepdims=True)
            gacc[STEP_ROW] += jnp.sum(value, axis=0, keepdims=True) * flag
            res[layer, rows, :] = jnp.where(masked, 0.0, value)

        for_rows(body)
        pltpu.make_async_copy(res.at[layer], gin.at[layer], gin_sem.at[turn]).start()
    for turn, layer in enumerate((other, own)):
        slot = 1 - turn
        pltpu.make_async_copy(gs.at[slot], ga.at[layer], gs_sem.at[slot]).wait()
        pltpu.make_async_copy(res.at[layer], gin.at[layer], gin_sem.at[turn]).wait()
    store_down.wait()
    send_memory.wait()


def run_pair(x2, cot2, aux, vec, wa, wu, wd):
    _, length, features = x2.shape
    hidden = wu.shape[2]
    blocks = length // RB
    pairs = features // LANES
    hbm = pl.BlockSpec(memory_space=pl.ANY)
    vmem = pl.BlockSpec(memory_space=pltpu.VMEM)
    dma = pltpu.SemaphoreType.DMA
    return pl.pallas_call(
        kernel,
        name="pair",
        out_shape=[
            jax.ShapeDtypeStruct(x2.shape, BF),
            jax.ShapeDtypeStruct(x2.shape, F32),
            jax.ShapeDtypeStruct(wa.shape, BF),
            jax.ShapeDtypeStruct(wu.shape, BF),
            jax.ShapeDtypeStruct(wd.shape, BF),
            jax.ShapeDtypeStruct(vec.shape, F32),
            jax.ShapeDtypeStruct((3, pairs * blocks, length, features), BF),
            jax.ShapeDtypeStruct((2, hidden // features, 2, length, features), BF),
        ],
        in_specs=[hbm, hbm, vmem, vmem, vmem, vmem, vmem],
        out_specs=[hbm] * 5 + [vmem] + [hbm] * 2,
        scratch_shapes=[
            pltpu.VMEM((2, length, features), BF),
            pltpu.VMEM((3, length, 3 * features), BF),
            pltpu.VMEM((3, length, features), BF),
            pltpu.VMEM((5, length, features), BF),
            pltpu.VMEM((5, length, 1), F32),
            pltpu.VMEM((4, length, features), BF),
            pltpu.VMEM((2, length, features), F32),
            pltpu.VMEM((length, features), BF),
            pltpu.VMEM((length, features), BF),
            pltpu.VMEM((length, features), BF),
            pltpu.VMEM((4, length, features), BF),
            pltpu.VMEM((length, features), BF),
            pltpu.VMEM((2, LANES, length), F32),
            pltpu.VMEM((2, features, hidden), BF),
            pltpu.VMEM((hidden, features), BF),
            dma,
            dma((2,)),
            dma((4,)),
            dma((2,)),
            dma,
            dma((2,)),
            dma((2,)),
        ],
        compiler_params=pltpu.CompilerParams(
            vmem_limit_bytes=64 << 20, has_side_effects=True
        ),
    )(x2, cot2, aux, vec, wa, wu, wd)


def per_device(
    tokens, cotangent, route, remask, timestep,
    enc_qkv, enc_out, enc_up, enc_down, enc_gains, enc_shifts,
    dec_qkv, dec_out, cross_query, cross_kv, cross_out, dec_up, dec_down, dec_gains, dec_shifts,
    time_table, mask_embed,
):
    sections = lax.axis_size("section")
    half = sections // 2
    shards = lax.axis_size("shard")
    section = lax.axis_index("section")
    shard = lax.axis_index("shard")
    role = (section >= half).astype(jnp.int32)
    batches, length, features = tokens.shape
    pair_row = ((section - half * role) * shards + shard) * batches + role
    steps = time_table.shape[0]

    def one(array, index):
        return lax.dynamic_index_in_dim(array, index, 0, keepdims=False)

    counts = jnp.sum(route.reshape(-1, batches, length).astype(F32), axis=(0, 2))
    total_tokens = float(route.shape[0] // batches * length)
    scale = one(route, pair_row).astype(F32) * total_tokens / one(counts, role)
    masked = one(remask, pair_row).astype(F32)
    lane = lax.broadcasted_iota(jnp.int32, (length, LANES), 1)
    aux = jnp.where(lane == 0, masked[:, None], jnp.where(lane == 1, scale[:, None], 0.0))

    swap = [(i, (i + half) % sections) for i in range(sections)]

    def swapped(array):
        return lax.ppermute(array, "section", swap)

    def both(array):
        mine = one(array, role)
        theirs = swapped(one(array, 1 - role))
        return jnp.stack([jnp.where(role == 0, mine, theirs), jnp.where(role == 0, theirs, mine)])

    x2, cot2 = both(tokens), both(cotangent)

    small = jnp.concatenate(
        [enc_gains, enc_shifts, dec_gains, dec_shifts, mask_embed[None, :], time_table], axis=0
    ).astype(BF)
    small = lax.all_gather(small, "shard", axis=1, tiled=True).astype(F32)
    step = one(timestep, pair_row)
    vec = jnp.concatenate([small[: MASK_ROW + 1], one(small, MASK_ROW + 1 + step)[None]], axis=0)
    wa = jnp.stack(
        [
            jnp.concatenate([enc_qkv, enc_out], axis=1),
            jnp.concatenate([dec_qkv, dec_out], axis=1),
            jnp.concatenate([cross_query, cross_kv, cross_out], axis=1),
        ]
    ).astype(BF)
    wu = jnp.stack([enc_up, dec_up]).astype(BF)
    wd = jnp.stack([enc_down, dec_down]).astype(BF)

    def gathered(array):
        return lax.all_gather(array, "shard", axis=1, tiled=True)

    lo, gin, ga, gu, gd, gacc, _, _ = run_pair(
        x2, cot2, aux, vec[:, None, :], gathered(wa), gathered(wu), gathered(wd)
    )

    def back(array):
        mine = one(array, role)
        theirs = swapped(one(array, 1 - role))
        return jnp.stack([jnp.where(role == 0, mine, theirs), jnp.where(role == 0, theirs, mine)])

    layer_out = back(lo)
    grad_in = back(gin)

    def reduced(array, axis):
        owned = lax.psum_scatter(array, "shard", scatter_dimension=axis, tiled=True)
        return lax.psum(owned.astype(F32), "section")

    ga, gu, gd = reduced(ga, 1), reduced(gu, 1), reduced(gd, 1)
    gacc = gacc[:, 0, :]
    picked = (jnp.arange(steps) == step).astype(F32)
    table = picked[:, None] * gacc[STEP_ROW][None, :]
    gv = reduced(jnp.concatenate([gacc[: MASK_ROW + 1], table], axis=0), 1)
    d = features
    return (
        layer_out, grad_in,
        ga[0, :, : 3 * d], ga[0, :, 3 * d :], gu[0], gd[0], gv[0:2], gv[2:4],
        ga[1, :, : 3 * d], ga[1, :, 3 * d :],
        ga[2, :, :d], ga[2, :, d : 3 * d], ga[2, :, 3 * d :],
        gu[1], gd[1], gv[4:7], gv[7:10], gv[MASK_ROW + 1 :], gv[MASK_ROW],
    )


def solution(mesh):
    rows = P(("section", "shard"), None, None)
    first, second, copied = P("shard", None), P(None, "shard"), P()
    return jax.shard_map(
        per_device,
        mesh=mesh,
        in_specs=(rows, rows, copied, copied, copied)
        + (first,) * 4 + (second,) * 2 + (first,) * 7 + (second,) * 3 + (P("shard"),),
        out_specs=(rows, rows)
        + (first,) * 4 + (second,) * 2 + (first,) * 7 + (second,) * 3 + (P("shard"),),
        check_vma=False,
    )
```

time: 2660 us -> 994 us (0.37)
  waiting for transfers between devices: 1440 us -> 522 us
  matrix products: 476 us -> 0 us
  Pallas kernels: 0 us -> 242 us
  local copies, waits for them, and re-layouts: 179 us -> 22.9 us
  blocking collectives: 299 us -> 160 us
  other arithmetic: 133 us -> 19.9 us
  starting transfers between devices: 74.4 us -> 6.12 us
  loops' own time: 37 us -> 0 us
    ppermute x4, waiting for transfers between devices: 854 us -> 88.6 us  [swapped(): return lax.ppermute(array, 'section', swap)]
    dot_general x62 -> x0, matrix products: 439 us -> none  [the longest x4 102 us: one_block(): jnp.einsum('hqk,khd->qhd', grad_scores, key_heads, preferred_element_type...]
    pallas_call x0 -> x1, Pallas kernels: none -> 242 us  [run_pair(): pl.pallas_call(kernel, name='pair', out_shape=[jax.ShapeDtypeStruct(x2.sh...]
    reduce_scatter x11 -> x4, waiting for transfers between devices: 373 us -> 208 us  [reduced(): owned = lax.psum_scatter(array, 'shard', scatter_dimension=axis, tiled=True)]
    all_gather x10 -> x1, blocking collectives: 139 us -> 13.3 us  [per_device(): small = lax.all_gather(small, 'shard', axis=1, tiled=True).astype(F32)]
    ppermute x4, starting transfers between devices: 73.4 us -> 5.84 us  [swapped(): return lax.ppermute(array, 'section', swap)]
    all_gather x7 -> x3, waiting for transfers between devices: 160 us -> 224 us  [gathered(): return lax.all_gather(array, 'shard', axis=1, tiled=True)]
    while x272 -> x0, local copies, waits for them, and re-layouts: 57.2 us -> none
  transfers between devices with their start and end apart: 27 -> 11, of which waited for: 22 -> 9; matrix products, arithmetic and copies ran while one was open for 3% -> 3% of each run, Pallas kernels for 0% -> 0%
where the time goes in v1:
time: 994 us; the launch traced here: 990 us
  waiting for transfers between devices  522 us (53%)
  Pallas kernels  242 us (24%)
  blocking collectives  160 us (16%)
  local copies, waits for them, and re-layouts  22.9 us (2%)
  other arithmetic  19.9 us (2%)
  between operations  16.1 us (2%)
    pallas_call x1, Pallas kernels, run_pair(): pl.pallas_call(kernel, name='pair', out_shape=[jax.ShapeDtypeStruct(x2.sh...  242 us
    all_gather x3, waiting for transfers between devices, gathered(): return lax.all_gather(array, 'shard', axis=1, tiled=True)  224 us
    reduce_scatter x4, waiting for transfers between devices, reduced(): owned = lax.psum_scatter(array, 'shard', scatter_dimension=axis, tiled=True)  208 us
    psum x1, blocking collectives, reduced(): return lax.psum(owned.astype(F32), 'section')  147 us
    ppermute x4, waiting for transfers between devices, swapped(): return lax.ppermute(array, 'section', swap)  88.6 us
  transfers between devices with their start and end apart: 11, of which 9 were waited for; matrix products, arithmetic and copies ran while one was open for 3% of the time, Pallas kernels for 0%

profile of v1, /device:TPU:0, one launch (start us, length us, event | category | flops | bytes accessed | tf_op | source)
XLA Modules:
  0.0 989.6 jit_solution(71941368054058623)
XLA Ops:
  7.2 1.7 convert_bitcast_fusion.2
  8.9 1.1 pad_maximum_fusion.5
  11.0 1.1 pad_maximum_fusion.6
  13.8 1.3 pad_maximum_fusion.4
  16.0 1.0 dynamic-slice_bitcast_fusion.2
  17.1 3.0 collective-permute-start.1
  20.0 1.0 dynamic-slice_bitcast_fusion.3
  22.4 13.3 %all_gather.12 = bf16[61,512]{1,0:T(8,128)(2,1)S(1)} all-gather(bf16[61,128]{1,0:T(8,128)(2,1)S(1)} %concatenate.22), channel_id=1, replica_groups=mesh['section'=8,'shard'=4] {'shard'}, dimensions={1}, use_global_device_ids=true | all-gather | bytes 78080 | tf_op jit(solution)/shard_map/all_gather | solution.py:487
  40.5 1.1 select_select_fusion.aux
  41.6 2.7 collective-permute-done.1
  44.3 1.4 fusion.4
  45.7 20.2 %collective-permute-done = bf16[1024,512]{1,0:T(8,128)(2,1)S(1)} collective-permute-done((bf16[1024,512]{1,0:T(8,128)(2,1)}, bf16[1024,512]{1,0:T(8,128)(2,1)S(1)}, u32[]{:S(2)}, u32[]{:S(2)}) %collective-permute-start) | collective-permute-done | bytes 1048608 | tf_op jit(solution)/shard_map/ppermute | solution.py:475
  66.0 2.4 pad_maximum_fusion.1
  68.4 26.2 %all-gather.6.cloned.1.call-done.wu = bf16[2,512,2048]{2,1,0:T(8,128)(2,1)} async-done(((bf16[2,128,2048]{2,1,0:T(8,128)(2,1)}), bf16[2,512,2048]{2,1,0:T(8,128)(2,1)}) %all-gather.6.cloned.1.call-update) | async-done | bytes 4194320 | tf_op jit(solution)/shard_map/all_gather | solution.py:501
  94.6 81.6 %all-gather.8.cloned.1.call-done.wd = bf16[2,2048,512]{2,1,0:T(8,128)(2,1)} async-done(((bf16[2,512,512]{2,1,0:T(8,128)(2,1)}), bf16[2,2048,512]{2,1,0:T(8,128)(2,1)}) %all-gather.8.cloned.1.call-update) | async-done | bytes 4194320 | tf_op jit(solution)/shard_map/all_gather | solution.py:501
  176.2 116.1 %all-gather.4.cloned.1.call-done.wa = bf16[3,512,2048]{2,1,0:T(8,128)(2,1)} async-done(((bf16[3,128,2048]{2,1,0:T(8,128)(2,1)}), bf16[3,512,2048]{2,1,0:T(8,128)(2,1)}) %all-gather.4.cloned.1.call-update) | async-done | bytes 6291472 | tf_op jit(solution)/shard_map/all_gather | solution.py:501
  292.3 242.5 %pair.1 = (bf16[2,1024,512]{2,1,0:T(8,128)(2,1)}, f32[2,1024,512]{2,1,0:T(8,128)}, bf16[3,512,2048]{2,1,0:T(8,128)(2,1)}, bf16[2,512,2048]{2,1,0:T(8,128)(2,1)},...) custom-call(bf16[2,1024,512]{2,1,0:T(8,128)(2,1)} %get-tuple-element, ...), custom_call_target="tpu_custom_call" | custom-call | tf_op jit(solution)/shard_map/pair/pallas_call | solution.py:401
  536.0 3.3 dynamic-slice_bitcast_fusion
  539.3 1.5 collective-permute-start.3
  540.8 1.0 dynamic-slice_bitcast_fusion.1
  543.8 65.7 %collective-permute-done.2 = bf16[1024,512]{1,0:T(8,128)(2,1)S(1)} collective-permute-done((bf16[1024,512]{1,0:T(8,128)(2,1)}, bf16[1024,512]{1,0:T(8,128)(2,1)S(1)}, u32[]{:S(2)}, u32[]{:S(2)}) %collective-permute-start.2) | collective-permute-done | bytes 1048608 | tf_op jit(solution)/shard_map/ppermute | solution.py:475
  609.7 1.5 pad_maximum_fusion.3
  611.2 1.4 copy-done
  612.7 2.1 fusion
  614.8 2.5 pad_maximum_fusion
  617.2 72.2 %reduce-scatter.9.cloned.1.call-done = bf16[2,512,512]{2,1,0:T(8,128)(2,1)} async-done(((bf16[2,2048,512]{2,1,0:T(8,128)(2,1)}), bf16[2,512,512]{2,1,0:T(8,128)(2,1)}) %reduce-scatter.9.cloned.1.call-update) | async-done | bytes 1048592 | tf_op jit(solution)/shard_map/reduce_scatter | solution.py:516
  689.4 113.4 %reduce-scatter.5.cloned.1.call-done = bf16[3,128,2048]{2,1,0:T(8,128)(2,1)} async-done(((bf16[3,512,2048]{2,1,0:T(8,128)(2,1)}), bf16[3,128,2048]{2,1,0:T(8,128)(2,1)}) %reduce-scatter.5.cloned.1.call-update) | async-done | bytes 1572880 | tf_op jit(solution)/shard_map/reduce_scatter | solution.py:516
  802.9 22.6 %reduce-scatter.11.cloned.1.call-done = f32[61,128]{1,0:T(8,128)} async-done(((f32[61,512]{1,0:T(8,128)}), f32[61,128]{1,0:T(8,128)}) %reduce-scatter.11.cloned.1.call-update) | async-done | bytes 31248 | tf_op jit(solution)/shard_map/reduce_scatter | solution.py:516
  825.4 147.0 %all-reduce.2 = (f32[3,128,2048]{2,1,0:T(8,128)S(1)}, f32[2,128,2048]{2,1,0:T(8,128)}, f32[2,512,512]{2,1,0:T(8,128)}, f32[61,128]{1,0:T(8,128)S(1)}) all-reduce(bf16[3,128,2048]{2,1,0:T(8,128)(2,1)} %reduce-scatter.5.cloned.1.call-done, ...), channel_id=1, replica_groups=mesh['section'=8,'shard'=4] {'section'}, use_global_device_ids=true, to_apply=%region_3.4 | all-reduce | flops 1842816 | bytes 11072512 | tf_op jit(solution)/shard_map/psum | solution.py:517
  976.6 1.3 slice_bitcast_fusion.4
  978.7 1.5 slice_bitcast_fusion.1
  981.1 1.5 slice_bitcast_fusion
  (111 shorter events, 17.5 us)
Async XLA Ops:
  7.2 87.4 %all-gather.6.cloned.1.call-start = ((), (), s32[]{:S(2)}) async-start(), calls=%async_computation.5 | async-start | bytes 5242880 | tf_op jit(solution)/shard_map/all_gather | solution.py:501
  8.9 1.6 copy-start.7
  8.9 1.9 copy-start.8
  10.0 166.2 %all-gather.8.cloned.1.call-start = ((), (), s32[]{:S(2)}) async-start(), calls=%async_computation.6 | async-start | bytes 5242880 | tf_op jit(solution)/shard_map/all_gather | solution.py:501
  11.0 1.5 copy-start.15
  11.0 1.7 copy-start.11
  12.1 1.4 copy-start.10
  12.1 280.1 %all-gather.4.cloned.1.call-start = ((), (), s32[]{:S(2)}) async-start(), calls=%async_computation.4 | async-start | bytes 7864320 | tf_op jit(solution)/shard_map/all_gather | solution.py:501
  13.8 2.2 copy-start.1
  15.1 602.1 %reduce-scatter.7.cloned.1.call-start = ((), (), s32[]{:S(2)}) async-start(), calls=%async_computation.8 | async-start | bytes 5242880 | tf_op jit(solution)/shard_map/reduce_scatter | solution.py:516
  16.0 4.1 copy-start.2
  16.0 6.0 copy-start.23
  16.0 6.0 copy-start.21
  16.0 6.0 copy-start.22
  16.0 6.0 copy-start.19
  16.0 6.0 copy-start.20
  16.0 6.0 copy-start.17
  16.0 19.7 %copy-start.24 = (s32[32]{0:T(128)S(1)}, s32[32]{0:T(128)}, u32[]{:S(2)}) copy-start(s32[32]{0:T(128)} %param.26) | copy-start | bytes 388
  16.0 21.6 %copy-start.16 = (s32[32,1024]{1,0:T(8,128)S(1)}, s32[32,1024]{1,0:T(8,128)}, u32[]{:S(2)}) copy-start(s32[32,1024]{1,0:T(8,128)} %param.24) | copy-start | bytes 393220
  17.1 27.3 %collective-permute-start.1 = (bf16[1024,512]{1,0:T(8,128)(2,1)}, bf16[1024,512]{1,0:T(8,128)(2,1)}, u32[]{:S(2)}, u32[]{:S(2)}) collective-permute-start(bf16[1024,512]{1,0:T(8,128)(2,1)} %dynamic-slice_bitcast_fusion.2), channel_id=1, source_target_pairs={{0,16},{4,20},{8,24},{12,28},{16,0},{20,4},{24,8},{28,12},{1,17},{... | collective-permute-start | bytes 3145736 | tf_op jit(solution)/shard_map/ppermute | solution.py:475
  21.1 44.8 %collective-permute-start = (bf16[1024,512]{1,0:T(8,128)(2,1)}, bf16[1024,512]{1,0:T(8,128)(2,1)S(1)}, u32[]{:S(2)}, u32[]{:S(2)}) collective-permute-start(bf16[1024,512]{1,0:T(8,128)(2,1)} %dynamic-slice_bitcast_fusion.3), channel_id=1, source_target_pairs={{0,16},{4,20},{8,24},{12,28},{16,0},{20,4},{24,8},{28,12},{1,17},{... | collective-permute-start | bytes 3145736 | tf_op jit(solution)/shard_map/ppermute | solution.py:475
  41.6 24.2 %copy-start.3 = (bf16[2,1024,512]{2,1,0:T(8,128)(2,1)S(1)}, bf16[2,1024,512]{2,1,0:T(8,128)(2,1)}, u32[]{:S(2)}) copy-start(bf16[2,1024,512]{2,1,0:T(8,128)(2,1)} %param.22) | copy-start | bytes 6291460
  534.8 154.6 %reduce-scatter.9.cloned.1.call-start = ((), (), s32[]{:S(2)}) async-start(), calls=%async_computation.9 | async-start | bytes 5242880 | tf_op jit(solution)/shard_map/reduce_scatter | solution.py:516
  535.4 267.5 %reduce-scatter.5.cloned.1.call-start = ((), (), s32[]{:S(2)}) async-start(), calls=%async_computation.7 | async-start | bytes 7864320 | tf_op jit(solution)/shard_map/reduce_scatter | solution.py:516
  536.0 289.5 %reduce-scatter.11.cloned.1.call-start = ((), (), s32[]{:S(2)}) async-start(), calls=%async_computation.10 | async-start | bytes 163840 | tf_op jit(solution)/shard_map/reduce_scatter | solution.py:516
  536.0 4.8 copy-start.4
  539.3 3.7 copy-start.18
  539.3 71.9 %collective-permute-start.3 = (f32[1024,512]{1,0:T(8,128)}, f32[1024,512]{1,0:T(8,128)}, u32[]{:S(2)}, u32[]{:S(2)}) collective-permute-start(f32[1024,512]{1,0:T(8,128)} %dynamic-slice_bitcast_fusion), channel_id=1, source_target_pairs={{0,16},{4,20},{8,24},{12,28},{16,0},{20,4},{24,8},{28,12},{1,17},{... | collective-permute-start | bytes 6291464 | tf_op jit(solution)/shard_map/ppermute | solution.py:475
  541.8 67.8 %collective-permute-start.2 = (bf16[1024,512]{1,0:T(8,128)(2,1)}, bf16[1024,512]{1,0:T(8,128)(2,1)S(1)}, u32[]{:S(2)}, u32[]{:S(2)}) collective-permute-start(bf16[1024,512]{1,0:T(8,128)(2,1)} %dynamic-slice_bitcast_fusion.1), channel_id=1, source_target_pairs={{0,16},{4,20},{8,24},{12,28},{16,0},{20,4},{24,8},{28,12},{1,17},{... | collective-permute-start | bytes 3145736 | tf_op jit(solution)/shard_map/ppermute | solution.py:475
  609.7 3.0 copy-start
  976.6 2.2 copy-start.6
  978.7 2.3 copy-start.5
  (4 other events, 4.9 us)
Sparse Core Ops, SparseCore 0:
  10.2 84.4 all-gather.5
  96.8 79.3 all-gather.7
  178.3 113.8 all-gather.3
  534.9 74.9 reduce-scatter.6
  612.1 77.2 reduce-scatter.8
  691.6 111.2 reduce-scatter.4
  805.7 19.7 reduce-scatter.10

commit v2 on v1

--- a/solution.py
+++ b/solution.py
@@ -20,6 +20,8 @@
 MASK_ROW = 10
 STEP_ROW = 11
 VEC_ROWS = 12
+SMALL_ROWS = 64
+MESH = pl.DeviceIdType.MESH
 
 
 def dot(left, right, dims=NN):
@@ -64,10 +66,12 @@
 
 
 def kernel(
-    x_in, cot_in, aux, vec, wa, wu, wd,
-    lo, gin, ga, gu, gd, gacc, p_hbm, f_hbm,
+    x_in, cot_in, aux, small_in, pick, wa_in, wu_in, wd_in,
+    lo, gin, ga, gu, gd, gacc, p_hbm, f_hbm, cot_land, out_land, gin_land,
+    wa, wu, wd, small, vec,
     x, qkv, oa, xh, rs, hb, res, dfb, dob, cotb, big, dp, kvt, gs, gsd,
-    x_sem, cot_sem, big_sem, gs_sem, gsd_sem, lo_sem, gin_sem,
+    send_sem, recv_sem, own_sem, small_sem, swap_sem,
+    cot_sem, big_sem, gs_sem, gsd_sem, lo_sem, gin_sem,
 ):
     length, features = x.shape[1], x.shape[2]
     hidden = wu.shape[2]
@@ -77,6 +81,96 @@
     section = lax.axis_index("section")
     role = (section >= lax.axis_size("section") // 2).astype(jnp.int32)
     own, other = role, 1 - role
+    sections, shards = lax.axis_size("section"), lax.axis_size("shard")
+    shard = lax.axis_index("shard")
+    core = lax.rem(section, 2)
+    side = lax.rem(section // 2, 2)
+    quarter = 2 * core + side
+    core_peer = (section + 1 - 2 * core, shard)
+    side_peer = (section + 2 - 4 * side, shard)
+    half_peer = (section + (sections // 2) * (1 - 2 * role), shard)
+    turns = range(1, shards)
+
+    def later(k):
+        return lax.rem(shard + k, shards)
+
+    def part(ref, lead, cols):
+        if cols is None:
+            return ref.at[lead]
+        return ref.at[lead, :, cols]
+
+    items = [
+        (wa_in, wa, own, slice(0, 3 * width)),
+        (wa_in, wa, own, slice(3 * width, 4 * width)),
+        (wa_in, wa, other, slice(0, 4 * width)),
+        (wu_in, wu, 0, slice(0, hidden)),
+        (wd_in, wd, 0, slice(0, width)),
+        (wa_in, wa, 2, slice(0, 4 * width)),
+        (wu_in, wu, 1, slice(0, hidden)),
+        (wd_in, wd, 1, slice(0, width)),
+    ]
+
+    def remote(src, dst, sems, peer):
+        return pltpu.make_async_remote_copy(
+            src_ref=src, dst_ref=dst, send_sem=send_sem.at[sems], recv_sem=recv_sem.at[sems],
+            device_id=peer, device_id_type=MESH,
+        )
+
+    def piece(item, owner, first, count):
+        _, full, lead, cols = items[item]
+        size = full.shape[1] // (4 * shards)
+        start = pl.multiple_of(owner * (4 * size) + first * size, size)
+        return full.at[lead, pl.ds(start, count * size), cols]
+
+    def hop(item, stage, k):
+        if stage == 0:
+            source, full, lead, cols = items[item]
+            size = full.shape[1] // (4 * shards)
+            src = source.at[lead, pl.ds(pl.multiple_of(quarter * size, size), size), cols]
+            return src, piece(item, shard, quarter, 1), (section, later(k))
+        if stage == 1:
+            src = piece(item, later(k), quarter, 1)
+            return src, src, side_peer
+        src = piece(item, later(k), 2 * core, 2)
+        return src, src, core_peer
+
+    def arrival(item, stage, k):
+        if stage == 0:
+            return piece(item, later(shards - k), quarter, 1)
+        if stage == 1:
+            return piece(item, later(k), 2 * core + 1 - side, 1)
+        return piece(item, later(k), 2 - 2 * core, 2)
+
+    def send(item, stage):
+        for k in turns:
+            src, dst, peer = hop(item, stage, k)
+            remote(src, dst, (item, stage, k - 1), peer).start()
+
+    def take(item, stage):
+        for k in turns:
+            dst = arrival(item, stage, k)
+            remote(dst, dst, (item, stage, k - 1), core_peer).wait_recv()
+
+    def own_copy(item):
+        source, full, lead, cols = items[item]
+        size = full.shape[1] // shards
+        return pltpu.make_async_copy(
+            source.at[lead, :, cols],
+            full.at[lead, pl.ds(pl.multiple_of(shard * size, size), size), cols],
+            own_sem.at[item],
+        )
+
+    def small_copy(k):
+        return pltpu.make_async_remote_copy(
+            src_ref=small_in, dst_ref=small.at[shard], send_sem=small_sem.at[0, k - 1],
+            recv_sem=small_sem.at[1, k - 1], device_id=(section, later(k)), device_id_type=MESH,
+        )
+
+    def swap_copy(src, dst, index):
+        return pltpu.make_async_remote_copy(
+            src_ref=src, dst_ref=dst, send_sem=swap_sem.at[0, index], recv_sem=swap_sem.at[1, index],
+            device_id=half_peer, device_id_type=MESH,
+        )
 
     def for_rows(body):
         def step(r, carry):
@@ -108,7 +202,7 @@
 
     slots = big.shape[0]
 
-    def attend(which):
+    def attend(which, polls=()):
         source, target, saved = qkv.at[which], oa.at[which], p_hbm.at[which]
         steps = pairs * blocks
 
@@ -127,6 +221,9 @@
             @pl.when(t >= slots)
             def _():
                 store(t - slots).wait()
+
+            for when, act in polls:
+                pl.when(t == when)(act)
 
             low = low_half((RB, LANES))
             zero = jnp.zeros_like(q)
@@ -169,7 +266,7 @@
         slot = c % 2
         return pltpu.make_async_copy(f_hbm.at[layer, c], big.at[2 * slot : 2 * slot + 2], big_sem.at[slot])
 
-    def feed(layer, hb_at):
+    def feed(layer, hb_at, polls=()):
         for c in range(chunks):
             slot = c % 2
             cols = slice(c * width, (c + 1) * width)
@@ -185,6 +282,9 @@
 
             for_rows(body)
             feed_store(layer, c).start()
+            for when, act in polls:
+                if when == c:
+                    act()
         for c in range(chunks - 2, chunks):
             feed_store(layer, c).wait()
 
@@ -298,53 +398,167 @@
 
         for_rows(body)
 
-    load_x = pltpu.make_async_copy(x_in, x, x_sem)
+    barrier = pltpu.get_barrier_semaphore()
+    peers = [(section, later(k)) for k in turns] + [core_peer, side_peer, half_peer]
+    for peer in peers:
+        pl.semaphore_signal(barrier, inc=1, device_id=peer, device_id_type=MESH)
+    pl.semaphore_wait(barrier, len(peers))
+
+    for k in turns:
+        small_copy(k).start()
+    send(0, 0)
+    load_small = pltpu.make_async_copy(small_in, small.at[shard], small_sem.at[2, 0])
+    load_small.start()
+    load_x = pltpu.make_async_copy(x_in.at[own], x.at[own], cot_sem.at[0])
     load_x.start()
+    swap_x = swap_copy(x_in.at[other], x.at[own], 0)
+    swap_x.start()
+    for item in range(len(items)):
+        own_copy(item).start()
+    send(1, 0)
+    send(2, 0)
+    gacc[...] = jnp.zeros_like(gacc)
+    swap_cot = swap_copy(cot_in.at[other], cot_land.at[own], 1)
+    swap_cot.start()
+    load_cot = pltpu.make_async_copy(cot_in.at[own], cot_land.at[own], cot_sem.at[1])
+    load_small.wait()
+    for k in turns:
+        small_copy(k).wait_recv()
+    for owner in range(shards):
+        values = small[owner].astype(F32)
+        cols = slice(owner * LANES, (owner + 1) * LANES)
+        for row in range(MASK_ROW + 1):
+            vec[row, :, cols] = values[row : row + 1, :]
+        vec[STEP_ROW, :, cols] = jnp.sum(values * pick[...], axis=0, keepdims=True)
     load_x.wait()
-    gacc[...] = jnp.zeros_like(gacc)
-
-    for layer in (own, other):
-        embed(layer)
-        project(x.at[layer], wa.at[layer], qkv.at[layer], 0, 3)
-        attend(layer)
-        out_norm(layer, layer, layer, 4 * layer, 2 + 5 * layer, layer)
-
-    feed(0, 0)
+    embed(own)
+    take(0, 0)
+    send(0, 1)
+    send(3, 0)
+    take(0, 1)
+    send(0, 2)
+    own_copy(0).wait()
+    take(0, 2)
+    project(x.at[own], wa.at[own], qkv.at[own], 0, 3)
+    take(1, 0)
+    send(1, 1)
+
+    def poll_0():
+        take(1, 1)
+        send(1, 2)
+
+    def poll_1():
+        take(2, 0)
+        send(2, 1)
+        send(4, 0)
+
+    def poll_2():
+        take(2, 1)
+        send(2, 2)
+        send(5, 0)
+
+    attend(own, [(2, poll_0), (5, poll_1), (11, poll_2)])
+    own_copy(1).wait()
+    take(1, 2)
+    out_norm(own, own, own, 4 * own, 2 + 5 * own, own)
+    swap_copy(x_in.at[other], x.at[other], 0).wait_recv()
+    embed(other)
+    own_copy(2).wait()
+    take(2, 2)
+    project(x.at[other], wa.at[other], qkv.at[other], 0, 3)
+
+    def poll_3():
+        take(3, 0)
+        send(3, 1)
+        send(6, 0)
+
+    def poll_4():
+        take(3, 1)
+        send(3, 2)
+        take(4, 0)
+        send(4, 1)
+        send(7, 0)
+
+    def poll_5():
+        take(4, 1)
+        send(4, 2)
+
+    attend(other, [(1, poll_3), (7, poll_4), (13, poll_5)])
+    out_norm(other, other, other, 4 * other, 2 + 5 * other, other)
+    own_copy(3).wait()
+    own_copy(4).wait()
+    take(3, 2)
+    take(4, 2)
+    take(5, 0)
+    send(5, 1)
+
+    def poll_6():
+        take(5, 1)
+        send(5, 2)
+        take(6, 0)
+        send(6, 1)
+
+    feed(0, 0, [(1, poll_6)])
     final_norm(0, 2, 1, 3, hb.at[2])
-    send_memory = pltpu.make_async_copy(hb.at[2], lo.at[0], lo_sem.at[0])
-    send_memory.start()
-    load_cot = pltpu.make_async_copy(cot_in.at[1], cotb, cot_sem.at[1])
-    load_cot.start()
+    stage_memory = pltpu.make_async_copy(hb.at[2], out_land.at[0], lo_sem.at[0])
+    stage_memory.start()
+    own_copy(5).wait()
+    take(5, 2)
     project(hb.at[1], wa.at[2], qkv.at[2], 0, 1)
     project(hb.at[2], wa.at[2], qkv.at[2], 1, 3)
-    attend(2)
+
+    def poll_7():
+        take(6, 1)
+        send(6, 2)
+        take(7, 0)
+        send(7, 1)
+
+    def poll_8():
+        take(7, 1)
+        send(7, 2)
+
+    attend(2, [(1, poll_7), (8, poll_8)])
     out_norm(2, 1, 3, 5, 8, 3)
+    own_copy(6).wait()
+    own_copy(7).wait()
+    take(6, 2)
+    take(7, 2)
+    load_cot_1 = pltpu.make_async_copy(cot_land.at[1], cotb, cot_sem.at[0])
+    load_cot_0 = pltpu.make_async_copy(cot_land.at[0], cotb, cot_sem.at[0])
+    load_cot.start()
     feed(1, 3)
+    load_cot.wait()
+    swap_copy(cot_in.at[other], cot_land.at[other], 1).wait_recv()
+    load_cot_1.start()
     final_norm(1, 4, 6, 9, dob)
-    send_result = pltpu.make_async_copy(dob, lo.at[1], lo_sem.at[1])
-    send_result.start()
+    stage_memory.wait()
+    stage_result = pltpu.make_async_copy(dob, out_land.at[1], lo_sem.at[1])
+    stage_result.start()
 
     def result_upstream(rows):
         return cotb[rows, :].astype(F32) * aux[rows, 1:2]
 
-    load_cot.wait()
+    load_cot_1.wait()
     norm_back(result_upstream, 1, 4, 6, 9)
-    load_cot = pltpu.make_async_copy(cot_in.at[0], cotb, cot_sem.at[0])
-    load_cot.start()
+    load_cot_0.start()
+    stage_result.wait()
+    send_result = swap_copy(out_land.at[other], lo.at[own], 2)
+    send_result.start()
+    keep_result = pltpu.make_async_copy(out_land.at[own], lo.at[own], lo_sem.at[0])
+    keep_result.start()
     feed_back(1, 3, gs.at[0], gsd)
     store_up = pltpu.make_async_copy(gs.at[0], gu.at[1], gs_sem.at[0])
     store_down = pltpu.make_async_copy(gsd, gd.at[1], gsd_sem)
     store_up.start()
     store_down.start()
     norm_back(lambda rows: res[1, rows, :], 1, 3, 5, 8)
-    send_result.wait()
     out_back(2, gs.at[1])
     attend_back(2)
     grad_weight(gs.at[1], 0, 1, hb.at[1], 2)
     grad_weight(gs.at[1], 1, 3, hb.at[2], 2)
     store_cross = pltpu.make_async_copy(gs.at[1], ga.at[2], gs_sem.at[1])
     store_cross.start()
-    load_cot.wait()
+    load_cot_0.wait()
 
     def cross_body(rows):
         res[1, rows, :] += dot(qkv[2, rows, :width], wa[2, :, :width], NT)
@@ -378,42 +592,85 @@
             masked = aux[rows, 0:1] * flag > 0.5
             gacc[MASK_ROW] += jnp.sum(jnp.where(masked, value, 0.0), axis=0, keepdims=True)
             gacc[STEP_ROW] += jnp.sum(value, axis=0, keepdims=True) * flag
-            res[layer, rows, :] = jnp.where(masked, 0.0, value)
+            value = jnp.where(masked, 0.0, value)
+            res[layer, rows, :] = value
+            if turn == 0:
+                cotb[rows, :] = value.astype(BF)
 
         for_rows(body)
-        pltpu.make_async_copy(res.at[layer], gin.at[layer], gin_sem.at[turn]).start()
+        if turn == 0:
+            send_gin = swap_copy(cotb, gin_land, 3)
+            send_gin.start()
+        else:
+            keep_gin = pltpu.make_async_copy(res.at[layer], gin.at[layer], gin_sem.at[0])
+            keep_gin.start()
     for turn, layer in enumerate((other, own)):
         slot = 1 - turn
         pltpu.make_async_copy(gs.at[slot], ga.at[layer], gs_sem.at[slot]).wait()
-        pltpu.make_async_copy(res.at[layer], gin.at[layer], gin_sem.at[turn]).wait()
     store_down.wait()
-    send_memory.wait()
-
-
-def run_pair(x2, cot2, aux, vec, wa, wu, wd):
+    send_gin.wait()
+    load_gin = pltpu.make_async_copy(gin_land, dob, gin_sem.at[1])
+    load_gin.start()
+    load_gin.wait()
+
+    def widen(rows):
+        res[other, rows, :] = dob[rows, :].astype(F32)
+
+    for_rows(widen)
+    keep_other = pltpu.make_async_copy(res.at[other], gin.at[other], gin_sem.at[1])
+    keep_other.start()
+    keep_other.wait()
+    keep_gin.wait()
+    keep_result.wait()
+    send_result.wait()
+    swap_x.wait_send()
+    swap_cot.wait_send()
+    for k in turns:
+        small_copy(k).wait_send()
+    for item in range(len(items)):
+        for stage in range(3):
+            for k in turns:
+                src, dst, peer = hop(item, stage, k)
+                remote(src, dst, (item, stage, k - 1), peer).wait_send()
+
+
+def run_pair(x2, cot2, aux, small, pick, wa, wu, wd):
     _, length, features = x2.shape
+    shards = lax.axis_size("shard")
     hidden = wu.shape[2]
     blocks = length // RB
     pairs = features // LANES
     hbm = pl.BlockSpec(memory_space=pl.ANY)
     vmem = pl.BlockSpec(memory_space=pltpu.VMEM)
     dma = pltpu.SemaphoreType.DMA
+    full_a = (3, features, 4 * features)
+    full_u = (2, features, hidden)
+    full_d = (2, hidden, features)
+    out = jax.ShapeDtypeStruct
     return pl.pallas_call(
         kernel,
         name="pair",
         out_shape=[
-            jax.ShapeDtypeStruct(x2.shape, BF),
-            jax.ShapeDtypeStruct(x2.shape, F32),
-            jax.ShapeDtypeStruct(wa.shape, BF),
-            jax.ShapeDtypeStruct(wu.shape, BF),
-            jax.ShapeDtypeStruct(wd.shape, BF),
-            jax.ShapeDtypeStruct(vec.shape, F32),
-            jax.ShapeDtypeStruct((3, pairs * blocks, length, features), BF),
-            jax.ShapeDtypeStruct((2, hidden // features, 2, length, features), BF),
+            out(x2.shape, BF),
+            out(x2.shape, F32),
+            out(full_a, BF),
+            out(full_u, BF),
+            out(full_d, BF),
+            out((VEC_ROWS, 1, features), F32),
+            out((3, pairs * blocks, length, features), BF),
+            out((2, hidden // features, 2, length, features), BF),
+            out(x2.shape, BF),
+            out(x2.shape, BF),
+            out(x2.shape[1:], BF),
         ],
-        in_specs=[hbm, hbm, vmem, vmem, vmem, vmem, vmem],
-        out_specs=[hbm] * 5 + [vmem] + [hbm] * 2,
+        in_specs=[hbm, hbm, vmem, vmem, vmem, hbm, hbm, hbm],
+        out_specs=[hbm] * 5 + [vmem] + [hbm] * 5,
         scratch_shapes=[
+            pltpu.VMEM(full_a, BF),
+            pltpu.VMEM(full_u, BF),
+            pltpu.VMEM(full_d, BF),
+            pltpu.VMEM((shards, SMALL_ROWS, LANES), BF),
+            pltpu.VMEM((VEC_ROWS, 1, features), F32),
             pltpu.VMEM((2, length, features), BF),
             pltpu.VMEM((3, length, 3 * features), BF),
             pltpu.VMEM((3, length, features), BF),
@@ -429,7 +686,11 @@
             pltpu.VMEM((2, LANES, length), F32),
             pltpu.VMEM((2, features, hidden), BF),
             pltpu.VMEM((hidden, features), BF),
-            dma,
+            dma((8, 3, shards - 1)),
+            dma((8, 3, shards - 1)),
+            dma((8,)),
+            dma((3, shards - 1)),
+            dma((2, 4)),
             dma((2,)),
             dma((4,)),
             dma((2,)),
@@ -438,9 +699,9 @@
             dma((2,)),
         ],
         compiler_params=pltpu.CompilerParams(
-            vmem_limit_bytes=64 << 20, has_side_effects=True
+            vmem_limit_bytes=64 << 20, has_side_effects=True, collective_id=0
         ),
-    )(x2, cot2, aux, vec, wa, wu, wd)
+    )(x2, cot2, aux, small, pick, wa, wu, wd)
 
 
 def per_device(
@@ -469,24 +730,13 @@
     lane = lax.broadcasted_iota(jnp.int32, (length, LANES), 1)
     aux = jnp.where(lane == 0, masked[:, None], jnp.where(lane == 1, scale[:, None], 0.0))
 
-    swap = [(i, (i + half) % sections) for i in range(sections)]
-
-    def swapped(array):
-        return lax.ppermute(array, "section", swap)
-
-    def both(array):
-        mine = one(array, role)
-        theirs = swapped(one(array, 1 - role))
-        return jnp.stack([jnp.where(role == 0, mine, theirs), jnp.where(role == 0, theirs, mine)])
-
-    x2, cot2 = both(tokens), both(cotangent)
-
     small = jnp.concatenate(
         [enc_gains, enc_shifts, dec_gains, dec_shifts, mask_embed[None, :], time_table], axis=0
     ).astype(BF)
-    small = lax.all_gather(small, "shard", axis=1, tiled=True).astype(F32)
+    small = jnp.pad(small, ((0, SMALL_ROWS - small.shape[0]), (0, 0)))
     step = one(timestep, pair_row)
-    vec = jnp.concatenate([small[: MASK_ROW + 1], one(small, MASK_ROW + 1 + step)[None]], axis=0)
+    row = lax.broadcasted_iota(jnp.int32, (SMALL_ROWS, LANES), 0)
+    pick = (row == MASK_ROW + 1 + step).astype(F32)
     wa = jnp.stack(
         [
             jnp.concatenate([enc_qkv, enc_out], axis=1),
@@ -497,20 +747,9 @@
     wu = jnp.stack([enc_up, dec_up]).astype(BF)
     wd = jnp.stack([enc_down, dec_down]).astype(BF)
 
-    def gathered(array):
-        return lax.all_gather(array, "shard", axis=1, tiled=True)
-
-    lo, gin, ga, gu, gd, gacc, _, _ = run_pair(
-        x2, cot2, aux, vec[:, None, :], gathered(wa), gathered(wu), gathered(wd)
-    )
-
-    def back(array):
-        mine = one(array, role)
-        theirs = swapped(one(array, 1 - role))
-        return jnp.stack([jnp.where(role == 0, mine, theirs), jnp.where(role == 0, theirs, mine)])
-
-    layer_out = back(lo)
-    grad_in = back(gin)
+    layer_out, grad_in, ga, gu, gd, gacc = run_pair(
+        tokens, cotangent, aux, small, pick, wa, wu, wd
+    )[:6]
 
     def reduced(array, axis):
         owned = lax.psum_scatter(array, "shard", scatter_dimension=axis, tiled=True)

time: 994 us -> 817 us (0.82)
  waiting for transfers between devices: 522 us -> 297 us
  Pallas kernels: 242 us -> 305 us
  blocking collectives: 160 us -> 147 us
    all_gather x3 -> x0, waiting for transfers between devices: 224 us -> none  [gathered(): return lax.all_gather(array, 'shard', axis=1, tiled=True)]
    ppermute x4 -> x0, waiting for transfers between devices: 88.6 us -> none  [swapped(): return lax.ppermute(array, 'section', swap)]
    reduce_scatter x4, waiting for transfers between devices: 208 us -> 296 us  [reduced(): owned = lax.psum_scatter(array, 'shard', scatter_dimension=axis, tiled=True)]
    pallas_call x1, Pallas kernels: 242 us -> 305 us  [run_pair(): pl.pallas_call(kernel, name='pair', out_shape=[out(x2.shape, BF), out(x2....]
    all_gather x1 -> x0, blocking collectives: 13.3 us -> none  [per_device(): small = lax.all_gather(small, 'shard', axis=1, tiled=True).astype(F32)]
  transfers between devices with their start and end apart: 11 -> 4, of which waited for: 9 -> 4; matrix products, arithmetic and copies ran while one was open for 3% -> 0% of each run, Pallas kernels for 0% -> 0%
where the time goes in v2:
time: 817 us; the launch traced here: 811 us
  Pallas kernels  305 us (37%)
  waiting for transfers between devices  297 us (36%)
  blocking collectives  147 us (18%)
  other arithmetic  24 us (3%)
  local copies, waits for them, and re-layouts  22.9 us (3%)
  between operations  14.9 us (2%)
    pallas_call x1, Pallas kernels, run_pair(): pl.pallas_call(kernel, name='pair', out_shape=[out(x2.shape, BF), out(x2....  305 us
    reduce_scatter x4, waiting for transfers between devices, reduced(): owned = lax.psum_scatter(array, 'shard', scatter_dimension=axis, tiled=True)  296 us
    psum x1, blocking collectives, reduced(): return lax.psum(owned.astype(F32), 'section')  147 us
  transfers between devices with their start and end apart: 4, of which 4 were waited for; matrix products, arithmetic and copies ran while one was open for 0% of the time, Pallas kernels for 0%

profile of v2, /device:TPU:0, one launch (start us, length us, event | category | flops | bytes accessed | tf_op | source)
XLA Modules:
  0.0 811.2 jit_solution(15627833819403161115)
XLA Ops:
  7.8 1.2 dynamic_slice.18
  10.2 1.2 convert.62
  11.4 1.2 convert.63
  12.6 1.2 convert_bitcast_fusion.4
  13.7 1.0 convert_reduce_fusion
  14.7 1.3 convert.64
  16.0 1.2 convert.65
  17.2 1.4 dynamic-slice_convert_fusion
  19.3 2.0 multiply_divide_fusion
  21.3 1.3 convert.67
  22.7 1.0 convert.69
  23.6 1.0 convert.71
  24.6 1.1 convert.72
  25.8 1.6 convert.74
  27.5 3.0 concatenate.19
  31.4 1.1 pad_maximum_fusion.1.wu_in
  33.3 1.1 pad_maximum_fusion.2.wd_in
  34.5 1.3 pad_maximum_fusion.wa_in
  35.9 1.1 select_select_fusion.aux
  37.7 305.1 %pair.1 = (bf16[2,1024,512]{2,1,0:T(8,128)(2,1)}, f32[2,1024,512]{2,1,0:T(8,128)}, bf16[3,512,2048]{2,1,0:T(8,128)(2,1)}, bf16[2,512,2048]{2,1,0:T(8,128)(2,1)},...) custom-call(bf16[2,1024,512]{2,1,0:T(8,128)(2,1)} %x_in.1, ...), custom_call_target="tpu_custom_call" | custom-call | tf_op jit(solution)/shard_map/pair/pallas_call | solution.py:650
  345.8 80.1 %reduce-scatter.7.cloned.1.call-done = bf16[2,128,2048]{2,1,0:T(8,128)(2,1)} async-done(((bf16[2,512,2048]{2,1,0:T(8,128)(2,1)}), bf16[2,128,2048]{2,1,0:T(8,128)(2,1)}) %reduce-scatter.7.cloned.1.call-update) | async-done | bytes 1048592 | tf_op jit(solution)/shard_map/reduce_scatter | solution.py:755
  425.9 79.7 %reduce-scatter.9.cloned.1.call-done = bf16[2,512,512]{2,1,0:T(8,128)(2,1)} async-done(((bf16[2,2048,512]{2,1,0:T(8,128)(2,1)}), bf16[2,512,512]{2,1,0:T(8,128)(2,1)}) %reduce-scatter.9.cloned.1.call-update) | async-done | bytes 1048592 | tf_op jit(solution)/shard_map/reduce_scatter | solution.py:755
  505.6 113.6 %reduce-scatter.5.cloned.1.call-done = bf16[3,128,2048]{2,1,0:T(8,128)(2,1)} async-done(((bf16[3,512,2048]{2,1,0:T(8,128)(2,1)}), bf16[3,128,2048]{2,1,0:T(8,128)(2,1)}) %reduce-scatter.5.cloned.1.call-update) | async-done | bytes 1572880 | tf_op jit(solution)/shard_map/reduce_scatter | solution.py:755
  619.2 22.4 %reduce-scatter.11.cloned.1.call-done = f32[61,128]{1,0:T(8,128)} async-done(((f32[61,512]{1,0:T(8,128)}), f32[61,128]{1,0:T(8,128)}) %reduce-scatter.11.cloned.1.call-update) | async-done | bytes 31248 | tf_op jit(solution)/shard_map/reduce_scatter | solution.py:755
  641.7 146.9 %all-reduce.3 = (f32[3,128,2048]{2,1,0:T(8,128)S(1)}, f32[2,128,2048]{2,1,0:T(8,128)}, f32[2,512,512]{2,1,0:T(8,128)}, f32[61,128]{1,0:T(8,128)S(1)}) all-reduce(bf16[3,128,2048]{2,1,0:T(8,128)(2,1)} %reduce-scatter.5.cloned.1.call-done, ...), channel_id=1, replica_groups=mesh['section'=8,'shard'=4] {'section'}, use_global_device_ids=true, to_apply=%region_3.4 | all-reduce | flops 1842816 | bytes 11072512 | tf_op jit(solution)/shard_map/psum | solution.py:756
  791.7 1.0 slice_bitcast_fusion.7
  792.7 1.3 slice_bitcast_fusion.4
  794.9 1.5 slice_bitcast_fusion.1
  797.2 1.5 slice_bitcast_fusion
  799.5 1.3 copy.53
  800.9 1.6 copy-done
  802.5 2.0 copy.54
  (68 shorter events, 13.1 us)
Async XLA Ops:
  7.2 20.2 %copy-start.10 = (f32[128,1024]{1,0:T(8,128)S(1)}, f32[128,1024]{1,0:T(8,128)}, u32[]{:S(2)}) copy-start(f32[128,1024]{1,0:T(8,128)} %param.36) | copy-start | bytes 1572868
  7.2 418.7 %reduce-scatter.7.cloned.1.call-start = ((), (), s32[]{:S(2)}) async-start(), calls=%async_computation.5 | async-start | bytes 5242880 | tf_op jit(solution)/shard_map/reduce_scatter | solution.py:755
  18.7 8.7 %copy-start.8 = (f32[128,1536]{1,0:T(8,128)S(1)}, f32[128,1536]{1,0:T(8,128)}, u32[]{:S(2)}) copy-start(f32[128,1536]{1,0:T(8,128)} %param.27) | copy-start | bytes 2359300
  18.7 8.8 %copy-start.9 = (f32[128,1536]{1,0:T(8,128)S(1)}, f32[128,1536]{1,0:T(8,128)}, u32[]{:S(2)}) copy-start(f32[128,1536]{1,0:T(8,128)} %param.33) | copy-start | bytes 2359300
  24.6 6.6 copy-start.4
  24.6 6.6 copy-start.5
  31.2 1.3 copy-start.6
  31.2 1.9 copy-start.7
  33.1 1.2 copy-start.11
  34.5 1.4 copy-start.13
  34.5 1.4 copy-start.14
  34.5 1.4 copy-start.16
  34.5 1.3 copy-start.17
  34.5 2.5 copy-start.15
  342.8 162.8 %reduce-scatter.9.cloned.1.call-start = ((), (), s32[]{:S(2)}) async-start(), calls=%async_computation.6 | async-start | bytes 5242880 | tf_op jit(solution)/shard_map/reduce_scatter | solution.py:755
  343.6 275.7 %reduce-scatter.5.cloned.1.call-start = ((), (), s32[]{:S(2)}) async-start(), calls=%async_computation.4 | async-start | bytes 7864320 | tf_op jit(solution)/shard_map/reduce_scatter | solution.py:755
  343.6 0.7 copy-start.12
  344.3 297.4 %reduce-scatter.11.cloned.1.call-start = ((), (), s32[]{:S(2)}) async-start(), calls=%async_computation.7 | async-start | bytes 163840 | tf_op jit(solution)/shard_map/reduce_scatter | solution.py:755
  792.7 2.2 copy-start.3
  794.8 2.3 copy-start.2
  797.2 2.3 copy-start.1
  799.5 2.9 copy-start
Sparse Core Ops, SparseCore 0:
  342.9 82.9 reduce-scatter.6
  428.3 77.2 reduce-scatter.8
  507.9 111.2 reduce-scatter.4
  621.9 19.7 reduce-scatter.10

commit v3 on v2

--- a/solution.py
+++ b/solution.py
@@ -15,12 +15,14 @@
 NT = (((1,), (1,)), ((), ()))
 TN = (((0,), (0,)), ((), ()))
 RB = 256
+AB = 512
 LANES = 128
 WIDTH = 512
 MASK_ROW = 10
 STEP_ROW = 11
 VEC_ROWS = 12
 SMALL_ROWS = 64
+UNITS = 7
 MESH = pl.DeviceIdType.MESH
 
 
@@ -67,11 +69,12 @@
 
 def kernel(
     x_in, cot_in, aux, small_in, pick, wa_in, wu_in, wd_in,
-    lo, gin, ga, gu, gd, gacc, p_hbm, f_hbm, cot_land, out_land, gin_land,
+    lo, gin, gout, gv, p_hbm, f_hbm, cot_land, out_land, gin_land, h_land,
     wa, wu, wd, small, vec,
-    x, qkv, oa, xh, rs, hb, res, dfb, dob, cotb, big, dp, kvt, gs, gsd,
+    gacc, x, qkv, oa, xh, rs, hb, res, dfb, dob, big, dp, kvt, gs,
+    r0, r1, r2, r3s, r3r, sg, sgr, sgz,
     send_sem, recv_sem, own_sem, small_sem, swap_sem,
-    cot_sem, big_sem, gs_sem, gsd_sem, lo_sem, gin_sem,
+    cot_sem, h_sem, big_sem, lo_sem, gin_sem, rs_send, rs_recv, rs_keep, sg_send, sg_recv, free,
 ):
     length, features = x.shape[1], x.shape[2]
     hidden = wu.shape[2]
@@ -88,8 +91,13 @@
     quarter = 2 * core + side
     core_peer = (section + 1 - 2 * core, shard)
     side_peer = (section + 2 - 4 * side, shard)
-    half_peer = (section + (sections // 2) * (1 - 2 * role), shard)
     turns = range(1, shards)
+
+    def bit_peer(bit):
+        return (section + bit * (1 - 2 * lax.rem(section // bit, 2)), shard)
+
+    far_peers = [bit_peer(4 << b) for b in range((sections // 4).bit_length() - 1)]
+    half_peer = far_peers[-1]
 
     def later(k):
         return lax.rem(shard + k, shards)
@@ -179,6 +187,193 @@
 
         lax.fori_loop(0, blocks, step, 0)
 
+    lane_ids = lax.broadcasted_iota(jnp.int32, (RB, LANES), 1)
+
+    def keep_inverse(index, rows, inverse):
+        rs[rows, :] = jnp.where(lane_ids == index, inverse, rs[rows, :])
+
+    def kept_inverse(index, rows):
+        return jnp.sum(jnp.where(lane_ids == index, rs[rows, :], 0.0), axis=-1, keepdims=True)
+
+    piece_rows = features // shards // 4
+    far = len(far_peers)
+    AT_Z, AT_FAR, AT_SIDE, AT_CORE = 2, 2 + len(turns), 2 + len(turns) + far, 3 + len(turns) + far
+    FREE_Z, FREE_FAR = 2, 3
+
+    def reduce_copy(unit, stage, src, dst, peer):
+        return pltpu.make_async_remote_copy(
+            src_ref=src, dst_ref=dst, send_sem=rs_send.at[unit, stage], recv_sem=rs_recv.at[unit, stage],
+            device_id=peer, device_id_type=MESH,
+        )
+
+    def rows_of(first, count):
+        return pl.ds(pl.multiple_of(first * piece_rows, piece_rows), count * piece_rows)
+
+    def copy_core(unit):
+        return reduce_copy(unit, 0, gs.at[unit % 2, :, rows_of(2 - 2 * core, 2), :], r0.at[unit % 2], core_peer)
+
+    def copy_side(unit):
+        return reduce_copy(unit, 1, r0.at[unit % 2, :, rows_of(1 - side, 1), :], r1.at[unit % 2], side_peer)
+
+    def copy_z(unit, k):
+        return reduce_copy(
+            unit, AT_Z + k - 1, r1.at[unit % 2, later(k)], r2.at[unit % 2, k - 1], (section, later(k))
+        )
+
+    def far_unit(unit, b):
+        return 11 - unit if unit >= 5 and b == far - 1 else unit
+
+    def copy_far(unit, b):
+        there = far_unit(unit, b)
+        return pltpu.make_async_remote_copy(
+            src_ref=r3s.at[unit % 2], dst_ref=r3r.at[there % 2, b],
+            send_sem=rs_send.at[unit, AT_FAR + b], recv_sem=rs_recv.at[there, AT_FAR + b],
+            device_id=far_peers[b], device_id_type=MESH,
+        )
+
+    def start_far(unit, b):
+        if unit >= 2:
+            pl.semaphore_wait(free.at[FREE_FAR + b, far_unit(unit, b) % 2], 1)
+        copy_far(unit, b).start()
+
+    def out_rows(unit, first, count):
+        return gout.at[unit_at[unit], rows_of(first, count), :]
+
+    def copy_back_side(unit):
+        return reduce_copy(unit, AT_SIDE, r3s.at[unit % 2], out_rows(unit, quarter, 1), side_peer)
+
+    def copy_keep(unit):
+        return pltpu.make_async_copy(r3s.at[unit % 2], out_rows(unit, quarter, 1), rs_keep.at[unit % 2])
+
+    def copy_back_core(unit):
+        rows = out_rows(unit, 2 * core, 2)
+        return reduce_copy(unit, AT_CORE, rows, rows, core_peer)
+
+    unit_at = [4, 6, 2, 3, 5, other, own]
+
+    def gain_credit(unit, kind, peers_of):
+        if unit + 2 < UNITS:
+            for peer in peers_of:
+                pl.semaphore_signal(free.at[kind, unit % 2], inc=1, device_id=peer, device_id_type=MESH)
+
+    def spend_credit(unit, kind, count=1):
+        if unit >= 2:
+            pl.semaphore_wait(free.at[kind, unit % 2], count)
+
+    def sum_start(unit):
+        spend_credit(unit, 0)
+        copy_core(unit).start()
+
+    def sum_core(unit):
+        copy_core(unit).wait()
+
+        def add(block, carry):
+            mine = gs[unit % 2, block, rows_of(2 * core, 2), :].astype(F32)
+            r0[unit % 2, block] = (r0[unit % 2, block].astype(F32) + mine).astype(BF)
+            return carry
+
+        lax.fori_loop(0, shards, add, 0)
+        spend_credit(unit, 1)
+        copy_side(unit).start()
+
+    def sum_side(unit):
+        copy_side(unit).wait()
+
+        def add(block, carry):
+            mine = r0[unit % 2, block, rows_of(side, 1), :].astype(F32)
+            r1[unit % 2, block] = (r1[unit % 2, block].astype(F32) + mine).astype(BF)
+            return carry
+
+        lax.fori_loop(0, shards, add, 0)
+        gain_credit(unit, 0, [core_peer])
+        spend_credit(unit, FREE_Z, len(turns))
+        for k in turns:
+            copy_z(unit, k).start()
+
+    def sum_z(unit):
+        for k in turns:
+            copy_z(unit, k).wait()
+        total = r1[unit % 2, shard].astype(F32)
+        for k in turns:
+            total += r2[unit % 2, k - 1].astype(F32)
+        r3s[unit % 2] = total.astype(BF)
+        gain_credit(unit, 1, [side_peer])
+        gain_credit(unit, FREE_Z, [(section, later(k)) for k in turns])
+        start_far(unit, 0)
+
+    def sum_far(unit):
+        for b in range(far):
+            copy_far(unit, b).wait_send()
+            arrived = r3r.at[unit % 2, b]
+            reduce_copy(unit, AT_FAR + b, arrived, arrived, far_peers[b]).wait_recv()
+            total = r3s[unit % 2].astype(F32) + r3r[unit % 2, b].astype(F32)
+            r3s[unit % 2] = total.astype(BF)
+            gain_credit(unit, FREE_FAR + b, [far_peers[b]])
+            if b + 1 < far:
+                start_far(unit, b + 1)
+        copy_keep(unit).start()
+        copy_back_side(unit).start()
+
+    def sum_back(unit):
+        copy_keep(unit).wait()
+        copy_back_side(unit).wait_send()
+        arrived = out_rows(unit, 2 * core + 1 - side, 1)
+        reduce_copy(unit, AT_SIDE, arrived, arrived, side_peer).wait_recv()
+        copy_back_core(unit).start()
+
+    def sum_end(unit):
+        copy_back_core(unit).wait_send()
+        arrived = out_rows(unit, 2 - 2 * core, 2)
+        reduce_copy(unit, AT_CORE, arrived, arrived, core_peer).wait_recv()
+
+    small_peers = [core_peer, side_peer]
+
+    def copy_small(b):
+        src = sg if b < 2 else sg.at[shard]
+        dst = sgr.at[b] if b < 2 else sgz.at[len(turns) + b - 2]
+        peer = small_peers[b] if b < 2 else far_peers[b - 2]
+        return pltpu.make_async_remote_copy(
+            src_ref=src, dst_ref=dst, send_sem=sg_send.at[len(turns) + b],
+            recv_sem=sg_recv.at[len(turns) + b], device_id=peer, device_id_type=MESH,
+        )
+
+    def copy_small_z(k):
+        return pltpu.make_async_remote_copy(
+            src_ref=sg.at[later(k)], dst_ref=sgz.at[k - 1], send_sem=sg_send.at[k - 1],
+            recv_sem=sg_recv.at[k - 1], device_id=(section, later(k)), device_id_type=MESH,
+        )
+
+    def small_start():
+        for owner in range(shards):
+            cols = slice(owner * LANES, (owner + 1) * LANES)
+            rows = [gacc[row, :, cols] for row in range(MASK_ROW + 1)]
+            rest = jnp.zeros((SMALL_ROWS - MASK_ROW - 1, LANES), F32)
+            sg[owner] = jnp.concatenate(rows + [rest], axis=0) + pick[...] * gacc[STEP_ROW, :, cols]
+        copy_small(0).start()
+
+    def small_add(b):
+        copy_small(b).wait()
+        sg[...] += sgr[b]
+        if b == 0:
+            copy_small(1).start()
+        else:
+            for k in turns:
+                copy_small_z(k).start()
+
+    def small_z():
+        for k in turns:
+            copy_small_z(k).wait()
+        sg[shard] += sum(sgz[k - 1] for k in turns)
+        copy_small(2).start()
+
+    def small_far():
+        for b in range(far):
+            copy_small(2 + b).wait()
+            sg[shard] += sgz[len(turns) + b]
+            if b + 1 < far:
+                copy_small(3 + b).start()
+        gv[...] = sg[shard]
+
     def embed(layer):
         flag = layer.astype(F32)
 
@@ -200,48 +395,47 @@
 
             for_rows(body)
 
-    slots = big.shape[0]
+    queries = length // AB
 
     def attend(which, polls=()):
         source, target, saved = qkv.at[which], oa.at[which], p_hbm.at[which]
-        steps = pairs * blocks
+        steps = pairs * queries
 
         def store(t):
-            slot = lax.rem(t, slots)
-            return pltpu.make_async_copy(big.at[slot], saved.at[t], big_sem.at[slot])
+            slot = lax.rem(t, 2)
+            return pltpu.make_async_copy(big.at[pl.ds(2 * slot, 2)], saved.at[t], big_sem.at[slot])
 
         def step(t, carry):
-            hp, qb = t // blocks, lax.rem(t, blocks)
-            slot = lax.rem(t, slots)
-            rows = rows_at(qb)
+            hp, qb = t // queries, lax.rem(t, queries)
+            slot = lax.rem(t, 2)
+            rows = rows_at(qb, AB)
             q = source[rows, lanes_at(hp)] * jnp.asarray(0.125, BF)
             k = source[:, lanes_at(pairs + hp)]
             v = source[:, lanes_at(2 * pairs + hp)]
 
-            @pl.when(t >= slots)
+            @pl.when(t >= 2)
             def _():
-                store(t - slots).wait()
+                store(t - 2).wait()
 
             for when, act in polls:
                 pl.when(t == when)(act)
 
-            low = low_half((RB, LANES))
+            low = low_half((AB, LANES))
             zero = jnp.zeros_like(q)
+            scores = [dot(jnp.where(low if j == 0 else ~low, q, zero), k, NT) for j in range(2)]
             parts = []
             for j in range(2):
-                s = dot(jnp.where(low if j == 0 else ~low, q, zero), k, NT)
-                e = jnp.exp(s - jnp.max(s, axis=-1, keepdims=True))
-                total = jnp.sum(e, axis=-1, keepdims=True)
-                weights = (e * (1.0 / total)).astype(BF)
+                e = jnp.exp(scores[j] - jnp.max(scores[j], axis=-1, keepdims=True))
+                weights = (e * (1.0 / jnp.sum(e, axis=-1, keepdims=True))).astype(BF)
                 for h in range(2):
-                    big[slot, (2 * j + h) * RB : (2 * j + h + 1) * RB, :] = weights[:, h * width : (h + 1) * width]
+                    big[2 * slot + j, h * AB : (h + 1) * AB, :] = weights[:, h * width : (h + 1) * width]
                 parts.append(dot(weights, v))
             target[rows, lanes_at(hp)] = jnp.where(low, parts[0], parts[1]).astype(BF)
             store(t).start()
             return carry
 
         lax.fori_loop(0, steps, step, 0)
-        for t in range(steps - slots, steps):
+        for t in range(steps - 2, steps):
             store(t).wait()
 
     def out_norm(which, res_at, xh_at, gain_row, shift_row, hb_at):
@@ -250,7 +444,7 @@
             normal, inverse = norm_rows(value)
             result = normal * vec[gain_row] + vec[shift_row]
             xh[xh_at, rows, :] = normal.astype(BF)
-            rs[xh_at, rows, :] = inverse
+            keep_inverse(xh_at, rows, inverse)
             res[res_at, rows, :] = result
             hb[hb_at, rows, :] = result.astype(BF)
 
@@ -288,20 +482,24 @@
         for c in range(chunks - 2, chunks):
             feed_store(layer, c).wait()
 
-    def final_norm(layer, xh_at, gain_row, shift_row, target):
+    def final_norm(layer, xh_at, gain_row, shift_row, target, kept=None):
+        kept = xh.at[xh_at] if kept is None else kept
+
         def body(rows):
             normal, inverse = norm_rows(res[layer, rows, :])
-            xh[xh_at, rows, :] = normal.astype(BF)
-            rs[xh_at, rows, :] = inverse
+            kept[rows, :] = normal.astype(BF)
+            keep_inverse(xh_at, rows, inverse)
             target[rows, :] = (normal * vec[gain_row] + vec[shift_row]).astype(BF)
 
         for_rows(body)
 
-    def norm_back(load, res_at, xh_at, gain_row, shift_row):
+    def norm_back(load, res_at, xh_at, gain_row, shift_row, kept=None):
+        kept = xh.at[xh_at] if kept is None else kept
+
         def body(rows):
             upstream = load(rows)
-            normal = xh[xh_at, rows, :].astype(F32)
-            result = norm_rows_back(upstream, normal, rs[xh_at, rows, :], vec[gain_row])
+            normal = kept[rows, :].astype(F32)
+            result = norm_rows_back(upstream, normal, kept_inverse(xh_at, rows), vec[gain_row])
             gacc[gain_row] += jnp.sum(upstream * normal, axis=0, keepdims=True)
             gacc[shift_row] += jnp.sum(upstream, axis=0, keepdims=True)
             res[res_at, rows, :] = result
@@ -309,7 +507,7 @@
 
         for_rows(body)
 
-    def feed_back(layer, hb_at, up, down):
+    def feed_back(layer, hb_at, up, down, polls=()):
         feed_load(layer, 0).start()
         feed_load(layer, 1).start()
         for c in range(chunks):
@@ -324,30 +522,41 @@
                 res[layer, rows, :] += dot(grad, wu[layer, :, cols], NT)
 
             for_rows(body)
-            up[:, cols] = dot(hb[hb_at], dp[...], TN).astype(BF)
-            down[cols, :] = dot(big[2 * slot], dfb[...], TN).astype(BF)
+            by_owner(up, cols, dot(hb[hb_at], dp[...], TN))
+            rest = dot(big[2 * slot], dfb[...], TN).astype(BF)
+            count = width // shards
+            for j in range(shards):
+                down[c, :, j * width : (j + 1) * width] = rest[j * count : (j + 1) * count, :]
             if c + 2 < chunks:
                 feed_load(layer, c + 2).start()
-
-    def attend_back(which):
+            for when, act in polls:
+                if when == c:
+                    act()
+
+    def by_owner(target, cols, value):
+        target[:, :, cols] = value.astype(BF).reshape(shards, features // shards, -1)
+
+    def attend_back(which, polls=()):
         source, output, saved = qkv.at[which], oa.at[which], p_hbm.at[which]
-        steps = pairs * blocks
+        steps = pairs * queries
 
         def fetch(t):
-            slot = lax.rem(t, slots)
-            return pltpu.make_async_copy(saved.at[t], big.at[slot], big_sem.at[slot])
-
-        for t in range(slots - 1):
-            fetch(t).start()
+            slot = lax.rem(t, 2)
+            return pltpu.make_async_copy(saved.at[t], big.at[pl.ds(2 * slot, 2)], big_sem.at[slot])
+
+        fetch(0).start()
 
         def step(t, carry):
-            hp, qb = t // blocks, lax.rem(t, blocks)
-            slot = lax.rem(t, slots)
-            rows = rows_at(qb)
-
-            @pl.when(t + slots - 1 < steps)
+            hp, qb = t // queries, lax.rem(t, queries)
+            slot = lax.rem(t, 2)
+            rows = rows_at(qb, AB)
+
+            @pl.when(t + 1 < steps)
             def _():
-                fetch(t + slots - 1).start()
+                fetch(t + 1).start()
+
+            for when, act in polls:
+                pl.when(t == when)(act)
 
             fetch(t).wait()
 
@@ -360,7 +569,7 @@
             v = source[:, lanes_at(2 * pairs + hp)]
             do = dob[rows, lanes_at(hp)]
             inner = do.astype(F32) * output[rows, lanes_at(hp)].astype(F32)
-            low = low_half((RB, LANES))
+            low = low_half((AB, LANES))
             zero = jnp.zeros_like(q)
             parts = []
             for j in range(2):
@@ -368,7 +577,7 @@
                 dom = jnp.where(mine, do, zero)
                 delta = jnp.sum(jnp.where(mine, inner, 0.0), axis=-1, keepdims=True)
                 weights = jnp.concatenate(
-                    [big[slot, (2 * j + h) * RB : (2 * j + h + 1) * RB, :] for h in range(2)], axis=1
+                    [big[2 * slot + j, h * AB : (h + 1) * AB, :] for h in range(2)], axis=1
                 )
                 ds = (weights.astype(F32) * (dot(dom, v, NT) - delta)).astype(BF)
                 kvt[1] += dot(dom, weights, TN)
@@ -376,7 +585,7 @@
                 parts.append(dot(ds, k))
             source[rows, lanes_at(hp)] = (jnp.where(low, parts[0], parts[1]) * 0.125).astype(BF)
 
-            @pl.when(qb == blocks - 1)
+            @pl.when(qb == queries - 1)
             def _():
                 source[:, lanes_at(pairs + hp)] = jnp.transpose(kvt[0] * 0.125).astype(BF)
                 source[:, lanes_at(2 * pairs + hp)] = jnp.transpose(kvt[1]).astype(BF)
@@ -388,10 +597,12 @@
     def grad_weight(target, first, last, left, which):
         for c in range(first, last):
             cols = slice(c * width, (c + 1) * width)
-            target[:, cols] = dot(left[...], qkv[which, :, cols], TN).astype(BF)
-
-    def out_back(which, target):
-        target[:, 3 * width :] = dot(oa[which], dfb[...], TN).astype(BF)
+            by_owner(target, cols, dot(left[...], qkv[which, :, cols], TN))
+
+    def out_grad(which, target):
+        by_owner(target, slice(3 * width, 4 * width), dot(oa[which], dfb[...], TN))
+
+    def out_back(which):
 
         def body(rows):
             dob[rows, :] = dot(dfb[rows, :], wa[which, :, 3 * width :], NT).astype(BF)
@@ -399,7 +610,7 @@
         for_rows(body)
 
     barrier = pltpu.get_barrier_semaphore()
-    peers = [(section, later(k)) for k in turns] + [core_peer, side_peer, half_peer]
+    peers = [(section, later(k)) for k in turns] + [core_peer, side_peer] + far_peers
     for peer in peers:
         pl.semaphore_signal(barrier, inc=1, device_id=peer, device_id_type=MESH)
     pl.semaphore_wait(barrier, len(peers))
@@ -457,7 +668,7 @@
         send(2, 2)
         send(5, 0)
 
-    attend(own, [(2, poll_0), (5, poll_1), (11, poll_2)])
+    attend(own, [(1, poll_0), (2, poll_1), (5, poll_2)])
     own_copy(1).wait()
     take(1, 2)
     out_norm(own, own, own, 4 * own, 2 + 5 * own, own)
@@ -483,7 +694,7 @@
         take(4, 1)
         send(4, 2)
 
-    attend(other, [(1, poll_3), (7, poll_4), (13, poll_5)])
+    attend(other, [(0, poll_3), (3, poll_4), (6, poll_5)])
     out_norm(other, other, other, 4 * other, 2 + 5 * other, other)
     own_copy(3).wait()
     own_copy(4).wait()
@@ -498,7 +709,11 @@
         take(6, 0)
         send(6, 1)
 
+    h_store = pltpu.make_async_copy(hb.at[0], h_land, h_sem)
+    h_load = pltpu.make_async_copy(h_land, hb.at[0], h_sem)
+    h_store.start()
     feed(0, 0, [(1, poll_6)])
+    h_store.wait()
     final_norm(0, 2, 1, 3, hb.at[2])
     stage_memory = pltpu.make_async_copy(hb.at[2], out_land.at[0], lo_sem.at[0])
     stage_memory.start()
@@ -517,75 +732,97 @@
         take(7, 1)
         send(7, 2)
 
-    attend(2, [(1, poll_7), (8, poll_8)])
-    out_norm(2, 1, 3, 5, 8, 3)
+    attend(2, [(0, poll_7), (4, poll_8)])
+    out_norm(2, 1, 3, 5, 8, 0)
     own_copy(6).wait()
     own_copy(7).wait()
     take(6, 2)
     take(7, 2)
-    load_cot_1 = pltpu.make_async_copy(cot_land.at[1], cotb, cot_sem.at[0])
-    load_cot_0 = pltpu.make_async_copy(cot_land.at[0], cotb, cot_sem.at[0])
+    load_cot_1 = pltpu.make_async_copy(cot_land.at[1], dp, cot_sem.at[0])
+    load_cot_0 = pltpu.make_async_copy(cot_land.at[0], dp, cot_sem.at[0])
     load_cot.start()
-    feed(1, 3)
+    feed(1, 0)
     load_cot.wait()
     swap_copy(cot_in.at[other], cot_land.at[other], 1).wait_recv()
     load_cot_1.start()
-    final_norm(1, 4, 6, 9, dob)
+    final_norm(1, 4, 6, 9, dob, big.at[3])
     stage_memory.wait()
     stage_result = pltpu.make_async_copy(dob, out_land.at[1], lo_sem.at[1])
     stage_result.start()
 
     def result_upstream(rows):
-        return cotb[rows, :].astype(F32) * aux[rows, 1:2]
+        return dp[rows, :].astype(F32) * aux[rows, 1:2]
 
     load_cot_1.wait()
-    norm_back(result_upstream, 1, 4, 6, 9)
-    load_cot_0.start()
+    norm_back(result_upstream, 1, 4, 6, 9, big.at[3])
     stage_result.wait()
     send_result = swap_copy(out_land.at[other], lo.at[own], 2)
     send_result.start()
     keep_result = pltpu.make_async_copy(out_land.at[own], lo.at[own], lo_sem.at[0])
     keep_result.start()
-    feed_back(1, 3, gs.at[0], gsd)
-    store_up = pltpu.make_async_copy(gs.at[0], gu.at[1], gs_sem.at[0])
-    store_down = pltpu.make_async_copy(gsd, gd.at[1], gsd_sem)
-    store_up.start()
-    store_down.start()
+    feed_back(1, 0, gs.at[0], gs.at[1])
+    h_load.start()
+    load_cot_0.start()
+    sum_start(0)
+    sum_start(1)
     norm_back(lambda rows: res[1, rows, :], 1, 3, 5, 8)
-    out_back(2, gs.at[1])
-    attend_back(2)
-    grad_weight(gs.at[1], 0, 1, hb.at[1], 2)
-    grad_weight(gs.at[1], 1, 3, hb.at[2], 2)
-    store_cross = pltpu.make_async_copy(gs.at[1], ga.at[2], gs_sem.at[1])
-    store_cross.start()
+    out_back(2)
+
+    def polls_of(*acts):
+        return [(when, functools.partial(act, unit)) for when, act, unit in acts]
+
+    attend_back(2, polls_of((0, sum_core, 0), (0, sum_core, 1), (3, sum_side, 0), (5, sum_side, 1)))
+    sum_z(0)
+    out_grad(2, gs.at[0])
+    grad_weight(gs.at[0], 0, 1, hb.at[1], 2)
+    grad_weight(gs.at[0], 1, 3, hb.at[2], 2)
+    sum_start(2)
     load_cot_0.wait()
 
     def cross_body(rows):
         res[1, rows, :] += dot(qkv[2, rows, :width], wa[2, :, :width], NT)
-        res[0, rows, :] = cotb[rows, :].astype(F32) + dot(
+        res[0, rows, :] = dp[rows, :].astype(F32) + dot(
             qkv[2, rows, width:], wa[2, :, width : 3 * width], NT
         )
 
     for_rows(cross_body)
+    sum_core(2)
     norm_back(lambda rows: res[0, rows, :], 0, 2, 1, 3)
-    store_up.wait()
-    store_down.wait()
-    feed_back(0, 0, gs.at[0], gsd)
-    store_up = pltpu.make_async_copy(gs.at[0], gu.at[0], gs_sem.at[0])
-    store_down = pltpu.make_async_copy(gsd, gd.at[0], gsd_sem)
-    store_up.start()
-    store_down.start()
-    store_cross.wait()
+    sum_z(1)
+    sum_far(0)
+    h_load.wait()
+    feed_back(
+        0, 0, gs.at[1], gs.at[0],
+        polls_of(
+            (0, sum_side, 2), (0, sum_far, 1), (0, sum_back, 0), (1, sum_back, 1), (1, sum_end, 0),
+            (2, sum_z, 2), (2, sum_end, 1),
+        ),
+    )
+    sum_start(3)
+    sum_start(4)
+    sum_far(2)
     for turn, layer in enumerate((other, own)):
-        slot = 1 - turn
+        unit = 5 + turn
+        slot = unit % 2
         flag = layer.astype(F32)
         norm_back(lambda rows: res[layer, rows, :], layer, layer, 4 * layer, 2 + 5 * layer)
-        if turn == 1:
-            store_up.wait()
-        out_back(layer, gs.at[slot])
-        attend_back(layer)
+        out_back(layer)
+        if turn == 0:
+            acts = polls_of(
+                (0, sum_core, 3), (0, sum_core, 4), (0, sum_back, 2), (2, sum_end, 2), (3, sum_side, 3),
+                (5, sum_side, 4), (6, sum_z, 3), (7, sum_far, 3),
+            )
+        else:
+            acts = polls_of(
+                (0, sum_back, 4), (1, sum_side, 5), (1, sum_end, 4), (4, sum_z, 5),
+            )
+        attend_back(layer, acts)
+        if turn == 0:
+            sum_z(4)
+            sum_back(3)
+        out_grad(layer, gs.at[slot])
         grad_weight(gs.at[slot], 0, 3, x.at[layer], layer)
-        pltpu.make_async_copy(gs.at[slot], ga.at[layer], gs_sem.at[slot]).start()
+        sum_start(unit)
 
         def body(rows):
             value = res[layer, rows, :] + dot(qkv[layer, rows, :], wa[layer, :, : 3 * width], NT)
@@ -595,19 +832,21 @@
             value = jnp.where(masked, 0.0, value)
             res[layer, rows, :] = value
             if turn == 0:
-                cotb[rows, :] = value.astype(BF)
+                dp[rows, :] = value.astype(BF)
 
         for_rows(body)
         if turn == 0:
-            send_gin = swap_copy(cotb, gin_land, 3)
+            send_gin = swap_copy(dp, gin_land, 3)
             send_gin.start()
+            sum_core(unit)
+            sum_far(4)
+            sum_end(3)
         else:
             keep_gin = pltpu.make_async_copy(res.at[layer], gin.at[layer], gin_sem.at[0])
             keep_gin.start()
-    for turn, layer in enumerate((other, own)):
-        slot = 1 - turn
-        pltpu.make_async_copy(gs.at[slot], ga.at[layer], gs_sem.at[slot]).wait()
-    store_down.wait()
+    small_start()
+    sum_core(6)
+    small_add(0)
     send_gin.wait()
     load_gin = pltpu.make_async_copy(gin_land, dob, gin_sem.at[1])
     load_gin.start()
@@ -619,6 +858,17 @@
     for_rows(widen)
     keep_other = pltpu.make_async_copy(res.at[other], gin.at[other], gin_sem.at[1])
     keep_other.start()
+    small_add(1)
+    sum_side(6)
+    small_z()
+    sum_z(6)
+    small_far()
+    sum_far(5)
+    sum_far(6)
+    sum_back(5)
+    sum_back(6)
+    sum_end(5)
+    sum_end(6)
     keep_other.wait()
     keep_gin.wait()
     keep_result.wait()
@@ -638,8 +888,9 @@
     _, length, features = x2.shape
     shards = lax.axis_size("shard")
     hidden = wu.shape[2]
-    blocks = length // RB
     pairs = features // LANES
+    quarters = features // shards
+    far = (lax.axis_size("section") // 4).bit_length() - 1
     hbm = pl.BlockSpec(memory_space=pl.ANY)
     vmem = pl.BlockSpec(memory_space=pltpu.VMEM)
     dma = pltpu.SemaphoreType.DMA
@@ -653,50 +904,61 @@
         out_shape=[
             out(x2.shape, BF),
             out(x2.shape, F32),
-            out(full_a, BF),
-            out(full_u, BF),
-            out(full_d, BF),
-            out((VEC_ROWS, 1, features), F32),
-            out((3, pairs * blocks, length, features), BF),
+            out((UNITS, features // shards, 4 * features), BF),
+            out((SMALL_ROWS, LANES), F32),
+            out((3, pairs * (length // AB), 2, length, features), BF),
             out((2, hidden // features, 2, length, features), BF),
             out(x2.shape, BF),
             out(x2.shape, BF),
             out(x2.shape[1:], BF),
+            out(x2.shape[1:], BF),
         ],
         in_specs=[hbm, hbm, vmem, vmem, vmem, hbm, hbm, hbm],
-        out_specs=[hbm] * 5 + [vmem] + [hbm] * 5,
+        out_specs=[hbm] * 3 + [vmem] + [hbm] * 6,
         scratch_shapes=[
             pltpu.VMEM(full_a, BF),
             pltpu.VMEM(full_u, BF),
             pltpu.VMEM(full_d, BF),
             pltpu.VMEM((shards, SMALL_ROWS, LANES), BF),
             pltpu.VMEM((VEC_ROWS, 1, features), F32),
+            pltpu.VMEM((VEC_ROWS, 1, features), F32),
             pltpu.VMEM((2, length, features), BF),
             pltpu.VMEM((3, length, 3 * features), BF),
             pltpu.VMEM((3, length, features), BF),
-            pltpu.VMEM((5, length, features), BF),
-            pltpu.VMEM((5, length, 1), F32),
             pltpu.VMEM((4, length, features), BF),
+            pltpu.VMEM((length, LANES), F32),
+            pltpu.VMEM((3, length, features), BF),
             pltpu.VMEM((2, length, features), F32),
-            pltpu.VMEM((length, features), BF),
             pltpu.VMEM((length, features), BF),
             pltpu.VMEM((length, features), BF),
             pltpu.VMEM((4, length, features), BF),
             pltpu.VMEM((length, features), BF),
             pltpu.VMEM((2, LANES, length), F32),
-            pltpu.VMEM((2, features, hidden), BF),
-            pltpu.VMEM((hidden, features), BF),
+            pltpu.VMEM((2, shards, quarters, hidden), BF),
+            pltpu.VMEM((2, shards, quarters // 2, hidden), BF),
+            pltpu.VMEM((2, shards, quarters // 4, hidden), BF),
+            pltpu.VMEM((2, shards - 1, quarters // 4, hidden), BF),
+            pltpu.VMEM((2, quarters // 4, hidden), BF),
+            pltpu.VMEM((2, far, quarters // 4, hidden), BF),
+            pltpu.VMEM((shards, SMALL_ROWS, LANES), F32),
+            pltpu.VMEM((2, shards, SMALL_ROWS, LANES), F32),
+            pltpu.VMEM((shards - 1 + far, SMALL_ROWS, LANES), F32),
             dma((8, 3, shards - 1)),
             dma((8, 3, shards - 1)),
             dma((8,)),
             dma((3, shards - 1)),
             dma((2, 4)),
             dma((2,)),
+            dma,
             dma((4,)),
             dma((2,)),
-            dma,
             dma((2,)),
+            dma((UNITS, 3 + shards + far)),
+            dma((UNITS, 3 + shards + far)),
             dma((2,)),
+            dma((shards + 1 + far,)),
+            dma((shards + 1 + far,)),
+            pltpu.SemaphoreType.REGULAR((3 + far, 2)),
         ],
         compiler_params=pltpu.CompilerParams(
             vmem_limit_bytes=64 << 20, has_side_effects=True, collective_id=0
@@ -747,26 +1009,21 @@
     wu = jnp.stack([enc_up, dec_up]).astype(BF)
     wd = jnp.stack([enc_down, dec_down]).astype(BF)
 
-    layer_out, grad_in, ga, gu, gd, gacc = run_pair(
+    layer_out, grad_in, gout, gv = run_pair(
         tokens, cotangent, aux, small, pick, wa, wu, wd
-    )[:6]
-
-    def reduced(array, axis):
-        owned = lax.psum_scatter(array, "shard", scatter_dimension=axis, tiled=True)
-        return lax.psum(owned.astype(F32), "section")
-
-    ga, gu, gd = reduced(ga, 1), reduced(gu, 1), reduced(gd, 1)
-    gacc = gacc[:, 0, :]
-    picked = (jnp.arange(steps) == step).astype(F32)
-    table = picked[:, None] * gacc[STEP_ROW][None, :]
-    gv = reduced(jnp.concatenate([gacc[: MASK_ROW + 1], table], axis=0), 1)
+    )[:4]
     d = features
+
+    def down(block):
+        return block.reshape(-1, shards, d).transpose(1, 0, 2).reshape(-1, d).astype(F32)
+
+    ga = [block.astype(F32) for block in gout[:5]]
     return (
         layer_out, grad_in,
-        ga[0, :, : 3 * d], ga[0, :, 3 * d :], gu[0], gd[0], gv[0:2], gv[2:4],
-        ga[1, :, : 3 * d], ga[1, :, 3 * d :],
-        ga[2, :, :d], ga[2, :, d : 3 * d], ga[2, :, 3 * d :],
-        gu[1], gd[1], gv[4:7], gv[7:10], gv[MASK_ROW + 1 :], gv[MASK_ROW],
+        ga[0][:, : 3 * d], ga[0][:, 3 * d :], ga[3], down(gout[5]), gv[0:2], gv[2:4],
+        ga[1][:, : 3 * d], ga[1][:, 3 * d :],
+        ga[2][:, :d], ga[2][:, d : 3 * d], ga[2][:, 3 * d :],
+        ga[4], down(gout[6]), gv[4:7], gv[7:10], gv[MASK_ROW + 1 : MASK_ROW + 1 + steps], gv[MASK_ROW],
     )
 
 

time: 817 us -> 443 us (0.54)
  waiting for transfers between devices: 297 us -> 0 us
  blocking collectives: 147 us -> 0 us
  Pallas kernels: 305 us -> 385 us
  between operations: 14.9 us -> 2.04 us
    reduce_scatter x4 -> x0, waiting for transfers between devices: 296 us -> none  [reduced(): owned = lax.psum_scatter(array, 'shard', scatter_dimension=axis, tiled=True)]
    psum x1 -> x0, blocking collectives: 147 us -> none  [reduced(): return lax.psum(owned.astype(F32), 'section')]
    pallas_call x1, Pallas kernels: 305 us -> 385 us  [run_pair(): pl.pallas_call(kernel, name='pair', out_shape=[out(x2.shape, BF), out(x2....]
  transfers between devices with their start and end apart: 4 -> 0, of which waited for: 4 -> 0; matrix products, arithmetic and copies ran while one was open for 0% -> 0% of each run, Pallas kernels for 0% -> 0%
where the time goes in v3:
time: 443 us; the launch traced here: 434 us
  Pallas kernels  385 us (87%)
  local copies, waits for them, and re-layouts  25.4 us (6%)
  other arithmetic  21.1 us (5%)
    pallas_call x1, Pallas kernels, run_pair(): pl.pallas_call(kernel, name='pair', out_shape=[out(x2.shape, BF), out(x2....  385 us

profile of v3, /device:TPU:0, one launch (start us, length us, event | category | flops | bytes accessed | tf_op | source)
XLA Modules:
  0.0 434.0 jit_solution(9216338020839852165)
XLA Ops:
  0.7 1.3 dynamic_slice.18
  4.7 1.0 convert_reduce_fusion
  7.1 0.8 dynamic-slice_convert_fusion
  8.6 1.4 multiply_divide_fusion
  10.0 0.8 convert.78
  12.4 1.0 convert.80
  13.4 1.0 convert.82
  14.4 1.0 convert.83
  15.4 1.0 convert.85
  16.7 1.3 pad_maximum_fusion.wa_in
  18.0 1.1 select_select_fusion.aux
  19.3 1.1 pad_maximum_fusion.1.wu_in
  21.2 1.1 pad_maximum_fusion.2.wd_in
  22.3 385.5 %pair.1 = (bf16[2,1024,512]{2,1,0:T(8,128)(2,1)}, f32[2,1024,512]{2,1,0:T(8,128)}, bf16[7,128,2048]{2,1,0:T(8,128)(2,1)}, f32[64,128]{1,0:T(8,128)}, bf16[3,8,2,...) custom-call(bf16[2,1024,512]{2,1,0:T(8,128)(2,1)} %x_in.1, ...), custom_call_target="tpu_custom_call" | custom-call | tf_op jit(solution)/shard_map/pair/pallas_call | solution.py:901
  407.8 1.2 slice_bitcast_fusion
  409.0 1.3 fusion.2
  410.3 1.3 fusion.1
  411.6 1.4 slice.64
  413.0 4.6 %slice_convert_fusion = (f32[1,128,2048]{2,1,0:T(8,128)}, f32[128,2048]{1,0:T(8,128)}, f32[128,2048]{1,0:T(8,128)S(1)}, f32[128,2048]{1,0:T(8,128)}, f32[1,128,2...) fusion(bf16[7,128,2048]{2,1,0:T(8,128)(2,1)} %get-tuple-element.25), kind=kLoop, calls=%fused_computation.11 | loop fusion | flops 1835008 | bytes 11010048 | tf_op jit(solution)/shard_map/convert_element_type | solution.py:1018
  417.6 1.9 reshape.88
  419.6 1.3 copy.44
  420.9 0.7 slice.69
  421.6 0.9 slice.68
  422.5 0.7 slice.67
  423.2 0.9 slice.66
  424.2 0.8 slice.71
  425.0 0.8 fusion
  425.9 0.7 reshape.87
  426.6 1.3 copy.43
  428.6 1.3 copy.47
  429.9 1.6 copy-done
  431.5 2.0 copy.48
  (41 shorter events, 7.7 us)
Async XLA Ops:
  0.7 15.7 %copy-start.10 = (f32[128,1024]{1,0:T(8,128)S(1)}, f32[128,1024]{1,0:T(8,128)}, u32[]{:S(2)}) copy-start(f32[128,1024]{1,0:T(8,128)} %param.36) | copy-start | bytes 1572868
  0.7 15.8 %copy-start.8 = (f32[128,1536]{1,0:T(8,128)S(1)}, f32[128,1536]{1,0:T(8,128)}, u32[]{:S(2)}) copy-start(f32[128,1536]{1,0:T(8,128)} %param.27) | copy-start | bytes 2359300
  13.4 3.2 copy-start.9
  16.7 2.5 copy-start.4
  16.7 2.5 copy-start.5
  19.2 1.3 copy-start.6
  19.2 1.9 copy-start.7
  419.5 1.3 copy-start.2
  419.5 3.0 copy-start.1
  426.6 2.0 copy-start.3
  428.5 2.9 copy-start
